TPU v7x, 256 devices: a whole 4x4x8 slice. The times are simulated.
256 devices in a mesh: seq: 32 (over z, x), vocab: 8 (over y, core).
Axes of the slice: x: 4, y: 4, z: 8, core: 2. Of those that a mesh axis runs over, the one named last changes fastest.
Arguments:
- hidden: bfloat16 [512, 5120], P(('seq', 'vocab')), may hold values from -400 to 400
- norm_gain: float32 [5120], replicated, may hold values from 0.1 to 1.9
- head_weight: bfloat16 [5120, 131072], P(None, ('seq', 'vocab')), may hold values from -2 to 2
- teacher_logits: bfloat16 [1024, 32, 4096], P('seq', None, 'vocab'), may hold values from -12 to 300
- teacher_slot: int32 [512], replicated, may hold values from 0 to 1023, as said below
- valid_tokens: int32 [512], replicated, may hold values 0 or 1
Outputs:
- grad_hidden: bfloat16 [512, 5120], P(('seq', 'vocab'))
- grad_head: bfloat16 [5120, 131072], P(None, ('seq', 'vocab'))
Inputs may be any that keep to these rules, and one draw needn't show every extreme that they name: `teacher_slot`: rows use distinct slots; slots g * 32 to (g + 1) * 32 - 1 belong to sequence group g of the teacher's packing; at most 32 rows use one group's slots, and some group holds 32 in every draw.
All inputs are finite; a program needn't handle non-finite values.
Results may differ from a plain program's by a relative error of at most 0.02.
Values may be sent and summed in bfloat16 or wider, within the bound.
A program may use at most 128 MiB of HBM per device.

v0:
```python
import jax
import jax.numpy as jnp
from jax import lax
from jax.sharding import PartitionSpec as P

epsilon = 1e-06


def shards(hidden, norm_gain, head_weight, teacher_logits, teacher_slot, valid_tokens):
    widened = hidden.astype(jnp.float32)
    inv_rms = lax.rsqrt(jnp.mean(widened * widened, axis=1, keepdims=True) + epsilon)
    normed = widened * inv_rms
    features = (normed * norm_gain).astype(jnp.bfloat16)
    gathered = lax.all_gather(features, ("seq", "vocab"), axis=0, tiled=True)
    logits = jnp.dot(gathered, head_weight, preferred_element_type=jnp.float32)
    arrived = lax.all_to_all(teacher_logits, "seq", split_axis=1, concat_axis=0, tiled=True)
    slot_table = arrived.reshape(arrived.shape[0], arrived.shape[2])
    teacher = jnp.take(slot_table, teacher_slot, axis=0).astype(jnp.float32)
    student_top, teacher_top = lax.pmax(
        (jnp.max(logits, axis=1), jnp.max(teacher, axis=1)), ("seq", "vocab")
    )
    shifted = jnp.exp(logits - student_top[:, None])
    teacher_shifted = jnp.exp(teacher - teacher_top[:, None])
    student_total, cross_sum, teacher_total = lax.psum(
        (
            jnp.sum(shifted, axis=1),
            jnp.sum(shifted * (logits - teacher), axis=1),
            jnp.sum(teacher_shifted, axis=1),
        ),
        ("seq", "vocab"),
    )
    student_lse = (student_top + jnp.log(student_total))[:, None]
    teacher_lse = (teacher_top + jnp.log(teacher_total))[:, None]
    divergence = cross_sum[:, None] / student_total[:, None] - student_lse + teacher_lse
    student_prob = jnp.exp(logits - student_lse)
    log_gap = logits - student_lse - (teacher - teacher_lse)
    row_weight = valid_tokens.astype(jnp.float32)[:, None]
    logit_grad = (row_weight * student_prob * (log_gap - divergence)).astype(jnp.bfloat16)
    grad_head = lax.dot_general(
        gathered, logit_grad, (((0,), (0,)), ((), ())), preferred_element_type=jnp.float32
    ).astype(jnp.bfloat16)
    feature_grad = lax.psum_scatter(
        lax.dot_general(
            logit_grad, head_weight, (((1,), (1,)), ((), ())), preferred_element_type=jnp.float32
        ),
        ("seq", "vocab"),
        scatter_dimension=0,
        tiled=True,
    )
    norm_grad = feature_grad * norm_gain
    grad_hidden = inv_rms * (
        norm_grad - normed * jnp.mean(norm_grad * normed, axis=1, keepdims=True)
    )
    return (grad_hidden.astype(jnp.bfloat16), grad_head)


def solution(mesh):
    placed = (
        P(("seq", "vocab"), None),
        P(),
        P(None, ("seq", "vocab")),
        P("seq", None, "vocab"),
        P(),
        P(),
    )
    return jax.shard_map(
        shards,
        mesh=mesh,
        in_specs=placed,
        out_specs=(P(("seq", "vocab"), None), P(None, ("seq", "vocab"))),
        check_vma=False,
    )
```

profile of v0, /device:TPU:1, one launch (start us, length us, event | category | flops | bytes accessed | tf_op | source)
XLA Modules:
  0.0 598.4 jit_solution(9775091275247822466)
XLA Ops:
  7.2 0.0 all-gather.3.cloned.1.call-start
  7.2 0.9 fusion.17
  8.1 1.4 fusion.19
  9.5 0.0 all-gather.3.cloned.1.call-update
  9.6 2.8 copy.10
  12.3 11.9 %all-to-all-start = ((bf16[32,32,512]{2,0,1:T(8,128)(2,1)}), bf16[32,32,512]{2,0,1:T(8,128)(2,1)S(1)}, u32[]{:S(2)}, u32[]{:S(2)}) async-start(bf16[32,32,512]{2,0,1:T(8,128)(2,1)} %copy.10), calls=%async_computation | async-start | bytes 2097152 | tf_op jit(solution)/shard_map/all_to_all | solution.py:16
  24.2 0.0 all-reduce.5.cloned.1.call-start
  24.3 0.7 convert_element_type.22
  25.0 0.7 compare_select_fusion
  25.6 0.7 compare_and_fusion
  26.3 24.3 %all-to-all-done = bf16[32,32,512]{2,0,1:T(8,128)(2,1)S(1)} async-done(((bf16[32,32,512]{2,0,1:T(8,128)(2,1)}), bf16[32,32,512]{2,0,1:T(8,128)(2,1)S(1)}, u32[]{:S(2)}, u32[]{:S(2)}) %all-to-all-start) | async-done | bytes 1048608 | tf_op jit(solution)/shard_map/all_to_all | solution.py:16
  50.7 2.0 gather_fusion
  52.6 0.2 copy.11
  52.8 0.2 fusion.9
  53.0 81.7 %all-gather.3.cloned.1.call-done = bf16[256,2,5120]{2,1,0:T(2,128)(2,1)} async-done(((bf16[1,2,5120]{2,1,0:T(2,128)(2,1)}), bf16[256,2,5120]{2,1,0:T(2,128)(2,1)}) %all-gather.3.cloned.1.call-update) | async-done | bytes 5242896 | tf_op jit(solution)/shard_map/all_gather | solution.py:14
  134.7 11.5 %reshape.46 = bf16[512,5120]{1,0:T(8,128)(2,1)} reshape(bf16[256,2,5120]{2,1,0:T(2,128)(2,1)} %all-gather.3.cloned.1.call-done) | data formatting | bytes 10485760
  146.1 7.2 %fusion.20 = (f32[512]{0:T(512)S(1)}, f32[512,512]{0,1:T(8,128)S(1)}) fusion(bf16[512,5120]{1,0:T(8,128)(2,1)} %reshape.46, bf16[5120,512]{1,0:T(8,128)(2,1)} %param.8), kind=kOutput, calls=%fused_computation.38 | convolution fusion | flops 2684616192 | bytes 11536384 | tf_op jit(solution)/shard_map/dot_general | solution.py:15
  153.3 75.1 %all-reduce.2 = (f32[512]{0:T(512)S(1)}, f32[512]{0:T(512)S(1)}) all-reduce(bf16[512]{0:T(512)(128)(2,1)S(1)} %fusion.9, f32[512]{0:T(512)S(1)} %get-tuple-element.13), channel_id=1, replica_groups=mesh['seq'=32,'vocab'=8] {'seq','vocab'}, use_global_device_ids=true, to_apply=%region_6.7 | all-reduce | flops 1024 | bytes 7168 | tf_op jit(solution)/shard_map/pmax | solution.py:19
  228.4 0.5 fusion.8
  228.9 73.1 %all-reduce.1 = (f32[512]{0:T(512)S(1)}, f32[512]{0:T(512)S(1)}, f32[512]{0:T(512)S(1)}) all-reduce(f32[512]{0:T(512)S(1)} %get-tuple-element.4, f32[512]{0:T(512)S(1)} %get-tuple-element.3, f32[512]{0:T(512)S(1)} %get-tuple-element.2), channel_id=1, replica_groups=mesh['seq'=32,'vocab'=8] {'seq','vocab'}, use_global_device_ids=true, to_apply=%region_8.9 | all-reduce | flops 1536 | bytes 12288 | tf_op jit(solution)/shard_map/psum | solution.py:24
  302.0 0.4 fusion.5
  302.4 8.0 %fusion.21 = f32[512,5120]{1,0:T(8,128)} fusion(bf16[512,512]{0,1:T(8,128)(2,1)S(1)} %fusion.5, bf16[5120,512]{1,0:T(8,128)(2,1)} %param.8), kind=kOutput, calls=%fused_computation.39 | convolution fusion | flops 2684354560 | bytes 16252928 | tf_op jit(solution)/shard_map/dot_general | solution.py:43
  310.3 0.0 all-reduce.5.cloned.1.call-update
  310.3 0.0 copy-start
  310.4 0.0 copy-start.1
  310.4 7.2 %convolution_convert_fusion = bf16[5120,512]{1,0:T(8,128)(2,1)} fusion(bf16[512,5120]{1,0:T(8,128)(2,1)} %reshape.46, bf16[512,512]{0,1:T(8,128)(2,1)S(1)} %fusion.5), kind=kOutput, calls=%fused_computation.1 | convolution fusion | flops 2686976000 | bytes 11010048 | tf_op jit(solution)/shard_map/dot_general | solution.py:39
  317.6 271.3 %all-reduce.5.cloned.1.call-done = f32[512,5120]{1,0:T(8,128)} async-done(((f32[512,5120]{1,0:T(8,128)}), f32[512,5120]{1,0:T(8,128)}) %all-reduce.5.cloned.1.call-update) | async-done | bytes 10485776
  588.8 0.0 copy-done
  588.8 0.0 copy-done.1
  588.8 1.1 fusion.14
  590.0 1.6 fusion.18
  (4 shorter events, 0.0 us)
Async XLA Ops:
  7.2 127.5 %all-gather.3.cloned.1.call-start = ((), (), s32[]{:S(2)}) async-start(), calls=%async_computation.1 | async-start | bytes 5263360 | tf_op jit(solution)/shard_map/all_gather | solution.py:14
  12.3 38.3 %all-to-all-start = ((bf16[32,32,512]{2,0,1:T(8,128)(2,1)}), bf16[32,32,512]{2,0,1:T(8,128)(2,1)S(1)}, u32[]{:S(2)}, u32[]{:S(2)}) async-start(bf16[32,32,512]{2,0,1:T(8,128)(2,1)} %copy.10), calls=%async_computation | async-start | bytes 2097152 | tf_op jit(solution)/shard_map/all_to_all | solution.py:16
  24.2 564.6 %all-reduce.5.cloned.1.call-start = ((), (), s32[]{:S(2)}) async-start(), calls=%async_computation.2 | async-start | bytes 20971520
  310.3 278.5 %copy-start = (bf16[2,5120]{1,0:T(2,128)(2,1)S(1)}, bf16[2,5120]{1,0:T(2,128)(2,1)}, u32[]{:S(2)}) copy-start(bf16[2,5120]{1,0:T(2,128)(2,1)} %param.6) | copy-start | bytes 61444
  310.4 278.5 %copy-start.1 = (f32[5120]{0:T(1024)S(1)}, f32[5120]{0:T(1024)}, u32[]{:S(2)}) copy-start(f32[5120]{0:T(1024)} %param.7) | copy-start | bytes 61444
Sparse Core Ops, SparseCore 0:
  12.3 122.3 all-gather.2
  310.5 278.3 all-reduce.4
where the time goes:
time: 600 us; the launch traced here: 598 us
  waiting for transfers between devices  377 us (63%)
  blocking collectives  148 us (25%)
  matrix products  22.4 us (4%)
  local copies, waits for them, and re-layouts  16.4 us (3%)
  between operations  14.1 us (2%)
  starting transfers between devices  11.9 us (2%)
  other arithmetic  8.17 us (1%)
    unnamed x3, waiting for transfers between devices  271 us
    all_gather x1, waiting for transfers between devices, shards(): gathered = lax.all_gather(features, ('seq', 'vocab'), axis=0, tiled=True)  81.7 us
    pmax x1, blocking collectives, shards(): lax.pmax((jnp.max(logits, axis=1), jnp.max(teacher, axis=1)), ('seq', 'vo...  75.1 us
    psum x1, blocking collectives, shards(): lax.psum((jnp.sum(shifted, axis=1), jnp.sum(shifted * (logits - teacher),...  73.1 us
    all_to_all x1, waiting for transfers between devices, shards(): lax.all_to_all(teacher_logits, 'seq', split_axis=1, concat_axis=0, tiled=...  24.3 us
    unnamed x6, local copies, waits for them, and re-layouts  14.2 us
  transfers between devices with their start and end apart: 3, of which 3 were waited for; matrix products, arithmetic and copies ran while one was open for 2% of the time, Pallas kernels for 0%

commit v1 on v0

v1 whole, which is shorter than its diff:
```python
import functools

import jax
import jax.numpy as jnp
from jax import lax
from jax.experimental import pallas as pl
from jax.experimental.pallas import tpu as pltpu
from jax.sharding import PartitionSpec as P

MESH = pl.DeviceIdType.MESH
F32 = jnp.float32
BF16 = jnp.bfloat16
epsilon = 1e-06

NZ, NX, NY, NC = 8, 4, 4, 2
NV, NS = NY * NC, NZ * NX
ROWS, D, CB, COLS = 512, 5120, 640, 512
NJ = 5
ORDER = (4, 0, 2, 1, 3)
XFIRST, YFIRST, ZFIRST = (0, 1), (2, 3), (4,)
N_SEM = 240


class Links:
    def __init__(self, send, recv):
        self.send, self.recv, self.used = send, recv, 0

    def take(self, count=1):
        first = self.used
        self.used += count
        assert self.used <= N_SEM
        return first

    def copy(self, src, dst, device, index=None):
        if index is None:
            index = self.take()
        return pltpu.make_async_remote_copy(
            src_ref=src,
            dst_ref=dst,
            send_sem=self.send.at[index],
            recv_sem=self.recv.at[index],
            device_id=device,
            device_id_type=MESH,
        )


def mod(value, n):
    return lax.rem(value, n)


def loop(count, body):
    def step(i, carry):
        body(i)
        return carry

    lax.fori_loop(0, count, step, 0)


def kernel(
    hid, gain, slot, valid, w_hbm, teach,
    gh_out, head_out,
    w, f, sf, rf, fa, t32, ts, tt, onehot, logits, trow, st, sa, sb, sc, grad,
    po, ps, cr, tx, rx, ty, ry, zr, ax, ay, az, t2, r2, tz2, rz2, a2, zz, a2z, yy, ra, sq, rq, stage,
    send, recv, wsem, osem,
):
    s = lax.axis_index("seq")
    v = lax.axis_index("vocab")
    z, x = lax.div(s, NX), mod(s, NX)
    y, c = lax.div(v, NC), mod(v, NC)
    links = Links(send, recv)

    def at_s(other):
        return (other, v)

    def at_v(other):
        return (s, other)

    def at_z(other):
        return (other * NX + x, v)

    def at_x(other):
        return (z * NX + other, v)

    def at_y(other):
        return (s, other * NC + c)

    wcopy = pltpu.make_async_copy(w_hbm, w, wsem)
    wcopy.start()

    barrier = pltpu.get_barrier_semaphore()

    def greet_seq(k):
        pl.semaphore_signal(barrier, inc=1, device_id=at_s(mod(s + k + 1, NS)), device_id_type=MESH)

    def greet_vocab(k):
        pl.semaphore_signal(barrier, inc=1, device_id=at_v(mod(v + k + 1, NV)), device_id_type=MESH)

    loop(NV - 1, greet_vocab)
    loop(NS - 1, greet_seq)

    h = hid[...].astype(F32)
    inv_rms = lax.rsqrt(jnp.mean(h * h, axis=1, keepdims=True) + epsilon)
    for b in range(NV):
        part = h[:, b * CB:(b + 1) * CB] * inv_rms * gain[b]
        sf[b] = part.astype(BF16).astype(F32)
    rf[v] = sf[v]
    pl.semaphore_wait(barrier, NV - 1 + NS - 1)

    first = links.take(NV)

    def block_copy(k):
        to = mod(v + k, NV)
        return links.copy(sf.at[to], rf.at[v], at_v(to), first + k)

    def block_arrival(k):
        source = mod(v + NV - k, NV)
        return links.copy(sf.at[source], rf.at[source], at_v(source), first + k)

    loop(NV - 1, lambda k: block_copy(k + 1).start())

    for b in range(4):
        t32[b] = teach[:, b * 128:(b + 1) * 128].astype(F32)
    teach_first = links.take(NS)

    def arrange(d):
        for b in range(4):
            ts[d, :, b * 128:(b + 1) * 128] = t32[b, pl.ds(d, 32, stride=NS), :].astype(BF16)

    loop(NS, arrange)

    loop(NV - 1, lambda k: block_arrival(k + 1).wait_recv())
    for b in range(NV):
        fa[2 * b:2 * b + 2, :] = rf[b]
    f[v, z, x] = fa[...].astype(BF16)

    z_first = links.take(NZ)

    def z_copy(k):
        return links.copy(f.at[v, z, x], f.at[v, z, x], at_z(mod(z + k, NZ)), z_first + k)

    def z_arrival(k):
        source = mod(z + NZ - k, NZ)
        return links.copy(f.at[v, source, x], f.at[v, source, x], at_z(source), z_first + k)

    loop(NZ - 1, lambda k: z_copy(k + 1).start())

    def teach_copy(k):
        to = mod(s + k, NS)
        return links.copy(ts.at[to], tt.at[s], at_s(to), teach_first + k)

    def teach_arrival(k):
        source = mod(s + NS - k, NS)
        return links.copy(ts.at[source], tt.at[source], at_s(source), teach_first + k)

    loop(NS - 1, lambda k: teach_copy(k + 1).start())
    tt[s] = ts[s]

    slot_column = jnp.broadcast_to(slot[...].astype(F32), (128, ROWS)).T
    lane = lax.broadcasted_iota(jnp.int32, (ROWS, 128), 1).astype(F32)
    for b in range(8):
        onehot[:, b * 128:(b + 1) * 128] = jnp.where(slot_column == lane + float(b * 128), 1.0, 0.0).astype(BF16)

    loop(NZ - 1, lambda k: z_arrival(k + 1).wait_recv())

    offsets = (0, 1, 3, 2)
    parts = [mod(x + NX - o, NX) for o in offsets]
    x_first = links.take(NX)

    def x_copy(o, part):
        return links.copy(f.at[v, :, part], f.at[v, :, part], at_x(mod(x + o, NX)), x_first + o)

    for o in (1, 3, 2):
        x_copy(o, x).start()
    up, down, far = mod(y + 1, NY), mod(y + 3, NY), mod(y + 2, NY)
    other_core = (s, y * NC + (1 - c))
    y_first = links.take(16)
    core_first = links.take(16)

    def y_copy(block_y, zs, part, to_y, index):
        ref = f.at[block_y * NC + c, zs[0]:zs[1], part]
        return links.copy(ref, ref, at_y(to_y), index)

    def core_send(rank, i, block_y):
        ref = f.at[block_y * NC + c, :, parts[i]]
        return links.copy(ref, ref, other_core, core_first + rank * 4 + i)

    def core_arrive(rank, i, block_y):
        ref = f.at[block_y * NC + 1 - c, :, parts[i]]
        return links.copy(ref, ref, other_core, core_first + rank * 4 + i)

    pending = []

    def go(copy):
        copy.start()
        pending.append(copy)

    for i, o in enumerate(offsets):
        if o:
            x_copy(o, parts[i]).wait_recv()
        go(y_copy(y, (0, NZ), parts[i], up, y_first + i))
        go(y_copy(y, (0, NZ), parts[i], down, y_first + 4 + i))
        go(core_send(0, i, y))
    for i in range(4):
        y_copy(down, (0, NZ), parts[i], up, y_first + i).wait_recv()
        go(y_copy(down, (0, 4), parts[i], up, y_first + 8 + i))
        go(core_send(1, i, down))
        y_copy(up, (0, NZ), parts[i], down, y_first + 4 + i).wait_recv()
        go(y_copy(up, (4, NZ), parts[i], down, y_first + 12 + i))
        go(core_send(2, i, up))

    wcopy.wait()

    def multiply(block_y, block_c, fresh=False):
        block = block_y * NC + block_c
        wb = w.at[block_y, block_c]

        def rows(i):
            fb = f[block, pl.ds(i * 4, 4)].reshape(256, CB)
            product = jnp.dot(fb, wb[...].reshape(CB, COLS), preferred_element_type=F32)
            span = pl.ds(pl.multiple_of(i * 256, 256), 256)
            if fresh:
                logits[span, :] = product
            else:
                logits[span, :] += product

        loop(2, rows)

    multiply(y, c, True)
    multiply(down, c)
    multiply(up, c)
    for i in range(4):
        y_copy(far, (0, 4), parts[i], up, y_first + 8 + i).wait_recv()
        y_copy(far, (4, NZ), parts[i], down, y_first + 12 + i).wait_recv()
        go(core_send(3, i, far))
    for rank, block_y in enumerate((y, down, up, far)):
        if rank == 3:
            multiply(far, c)
        for i in range(4):
            core_arrive(rank, i, block_y).wait_recv()
        multiply(block_y, 1 - c)

    loop(NS - 1, lambda k: teach_arrival(k + 1).wait_recv())

    def select(i):
        span = pl.ds(pl.multiple_of(i * 256, 256), 256)
        trow[span, :] = jnp.dot(onehot[span, :], tt[...].reshape(1024, COLS), preferred_element_type=F32)

    loop(2, select)

    def statistics(i):
        span = pl.ds(pl.multiple_of(i * 64, 64), 64)
        lo, te = logits[span, :], trow[span, :]
        top = jnp.max(lo, axis=1, keepdims=True)
        teacher_top = jnp.max(te, axis=1, keepdims=True)
        e = jnp.exp(lo - top)
        total = jnp.sum(e, axis=1, keepdims=True)
        cross = jnp.sum(e * (lo - te), axis=1, keepdims=True)
        teacher_total = jnp.sum(jnp.exp(te - teacher_top), axis=1, keepdims=True)
        column = lax.broadcasted_iota(jnp.int32, (64, 128), 1)
        packed = jnp.where(column == 0, top, jnp.where(column == 1, teacher_top, jnp.where(column == 2, total, jnp.where(
            column == 3, cross, jnp.where(column == 4, teacher_total, 0.0)))))
        st[span, :] = packed

    loop(8, statistics)

    def merged(ref):
        value = ref[...]
        top = jnp.max(value[:, 0:1, :], axis=0, keepdims=True)
        teacher_top = jnp.max(value[:, 1:2, :], axis=0, keepdims=True)
        scale = jnp.exp(value[:, 0:1, :] - top)
        teacher_scale = jnp.exp(value[:, 1:2, :] - teacher_top)
        total = jnp.sum(value[:, 2:3, :] * scale, axis=0)
        cross = jnp.sum(value[:, 3:4, :] * scale, axis=0)
        teacher_total = jnp.sum(value[:, 4:5, :] * teacher_scale, axis=0)
        return top[0], teacher_top[0], total, cross, teacher_total

    def exchange(buffer, here, count, device):
        start = links.take(count)

        def out(k):
            return links.copy(buffer.at[here], buffer.at[here], device(mod(here + k, count)), start + k)

        def arrival(k):
            source = mod(here + count - k, count)
            return links.copy(buffer.at[source], buffer.at[source], device(source), start + k)

        loop(count - 1, lambda k: out(k + 1).start())
        loop(count - 1, lambda k: arrival(k + 1).wait_recv())
        return lambda: loop(count - 1, lambda k: out(k + 1).wait_send())

    def put(buffer, here, rows):
        for r, row in enumerate(rows):
            buffer[here, r:r + 1, :] = row

    flushes = []
    sa[v] = st[...].T[0:8, :]
    flushes.append(exchange(sa, v, NV, at_v))
    put(sb, x, merged(sa))
    flushes.append(exchange(sb, x, NX, at_x))
    put(sc, z, merged(sb))
    flushes.append(exchange(sc, z, NZ, at_z))
    top, teacher_top, total, cross, teacher_total = merged(sc)
    student_lse = top + jnp.log(total)
    teacher_lse = teacher_top + jnp.log(teacher_total)
    divergence = cross / total - student_lse + teacher_lse
    quantity = lax.broadcasted_iota(jnp.int32, (128, ROWS), 0)
    st[...] = jnp.where(quantity == 0, student_lse, jnp.where(quantity == 1, teacher_lse, jnp.where(
        quantity == 2, divergence, valid[...].astype(F32)))).T

    def gradient(i):
        span = pl.ds(pl.multiple_of(i * 64, 64), 64)
        lo, te, q = logits[span, :], trow[span, :], st[span, :]
        shifted = lo - q[:, 0:1]
        gap = shifted - (te - q[:, 1:2])
        grad[span, :] = (q[:, 3:4] * jnp.exp(shifted) * (gap - q[:, 2:3])).astype(BF16)

    loop(8, gradient)

    def partial(j, half, ref):
        wj = w.at[:, half, j]

        def rows(i):
            g = grad[pl.ds(pl.multiple_of(i * 256, 256), 256), :]
            product = lax.dot_general(g, wj[...].reshape(4 * 128, COLS), (((1,), (1,)), ((), ())), preferred_element_type=F32)
            for b in range(NY):
                ref[j, b, pl.ds(i * 4, 4)] = product[:, b * 128:(b + 1) * 128].reshape(4, NX, 16, 128)

        loop(2, rows)

    def add_core(j):
        def step(i):
            ps[j, i] += cr[j, i]

        loop(NY, step)

    class Ring:
        def __init__(self, here, device, block, tmp, arrived):
            self.block, self.tmp, self.arrived, self.here = block, tmp, arrived, here
            up, down, far = mod(here + 1, 4), mod(here + 3, 4), mod(here + 2, 4)
            self.up, self.down = up, down
            self.far0 = links.copy(block(far, 0), tmp.at[0], device(up))
            self.far1 = links.copy(block(far, 1), tmp.at[1], device(down))
            self.free0 = links.copy(block(up, 1), arrived.at[0, 1], device(up))
            self.free1 = links.copy(block(down, 0), arrived.at[1, 0], device(down))
            self.last0 = links.copy(tmp.at[0], arrived.at[0, 0], device(up))
            self.last1 = links.copy(tmp.at[1], arrived.at[1, 1], device(down))
            for copy in (self.far0, self.far1, self.free0, self.free1):
                go(copy)

        def middle(self):
            self.far0.wait_recv()
            self.tmp[0] = self.tmp[0] + self.block(self.up, 0)[...]
            go(self.last0)
            self.far1.wait_recv()
            self.tmp[1] = self.tmp[1] + self.block(self.down, 1)[...]
            go(self.last1)

        def finish(self):
            for copy in (self.free0, self.free1, self.last0, self.last1):
                copy.wait_recv()
            return [self.block(self.here, i)[...] + self.arrived[0, i] + self.arrived[1, i] for i in (0, 1)]

    core_links = {j: links.copy(po.at[j], cr.at[j], other_core) for j in ORDER}
    stage1 = {}
    z_direct = links.take(NZ)

    def zr_copy(k):
        to = mod(z + k, NZ)
        return links.copy(ps.at[4, :, to], zr.at[z], at_z(to), z_direct + k)

    def zr_arrival(k):
        source = mod(z + NZ - k, NZ)
        return links.copy(ps.at[4, :, source], zr.at[source], at_z(source), z_direct + k)

    def begin(j):
        core_links[j].wait_recv()
        add_core(j)
        if j in XFIRST:
            stage1[j] = Ring(x, at_x, lambda i, half, j=j: ps.at[j, half * 2:half * 2 + 2, :, i], tx.at[j], rx.at[j])
        elif j in YFIRST:
            stage1[j] = Ring(y, at_y, lambda i, half, j=j: ps.at[j, i, half * 4:half * 4 + 4], ty.at[j - 2], ry.at[j - 2])
        else:
            loop(NZ - 1, lambda k: zr_copy(k + 1).start())

    for n, j in enumerate(ORDER):
        partial(j, 1 - c, po)
        go(core_links[j])
        partial(j, c, ps)
        if n:
            begin(ORDER[n - 1])
    begin(ORDER[-1])

    out_copies = [pltpu.make_async_copy(stage.at[b % 2], head_out.at[b], osem.at[b % 2]) for b in range(NV)]

    def head_block(b):
        if b >= 2:
            out_copies[b - 2].wait()

        fb = f[b].reshape(ROWS, CB)
        product = lax.dot_general(fb, grad[...], (((0,), (0,)), ((), ())), preferred_element_type=F32)
        stage[b % 2] = product.astype(BF16)
        out_copies[b].start()

    for b in range(4):
        head_block(b)
    for j in ORDER[1:]:
        stage1[j].middle()
    for b in range(4, NV):
        head_block(b)

    def spread(buffer, source, here, count, device):
        start = links.take(count)

        def out(k):
            to = mod(here + k, count)
            return links.copy(source.at[to], buffer.at[here], device(to), start + k)

        def arrival(k):
            other = mod(here + count - k, count)
            return links.copy(source.at[other], buffer.at[other], device(other), start + k)

        loop(count - 1, lambda k: out(k + 1).start())
        buffer[here] = source[here]
        flushes.append(lambda: loop(count - 1, lambda k: out(k + 1).wait_send()))
        return lambda: loop(count - 1, lambda k: arrival(k + 1).wait_recv())

    stage2, stage3 = {}, {}
    for j in ORDER[1:]:
        low, high = stage1[j].finish()
        if j in XFIRST:
            mine = ax.at[j]
            mine[0:2] = low
            mine[2:4] = high
            stage2[j] = Ring(y, at_y, lambda i, half, m=mine: m.at[i, half * 4:half * 4 + 4], t2.at[j], r2.at[j])
        else:
            mine = ay.at[j - 2]
            mine[0:4] = low
            mine[4:8] = high
            stage2[j] = Ring(x, at_x, lambda i, half, m=mine: m.at[half * 4:half * 4 + 4, i], t2.at[j], r2.at[j])
    loop(NZ - 1, lambda k: zr_arrival(k + 1).wait_recv())
    az[...] = ps[4, :, z]

    def add_z(k):
        az[...] += zr[mod(z + NZ - k - 1, NZ)]

    loop(NZ - 1, add_z)
    stage2[4] = Ring(x, at_x, lambda i, half: az.at[half * 2:half * 2 + 2, i], tz2, rz2)
    for j in (0, 2, 1, 3, 4):
        stage2[j].middle()
    for j in (0, 2, 1, 3, 4):
        low, high = stage2[j].finish()
        if j == 4:
            a2z[0:2] = low
            a2z[2:4] = high
            stage3[j] = spread(yy, a2z, y, NY, at_y)
        else:
            a2[j, 0:4] = low
            a2[j, 4:8] = high
            stage3[j] = spread(zz.at[j], a2.at[j], z, NZ, at_z)
    for j in (0, 2, 1, 3, 4):
        stage3[j]()
        arrived = yy[...] if j == 4 else zz[j]
        ra[:, j * 128:(j + 1) * 128] = jnp.sum(arrived, axis=0)
    for b in range(NV):
        sq[b] = ra[2 * b:2 * b + 2, :]
    spread(rq, sq, v, NV, at_v)()

    h = hid[...].astype(F32)
    inv_rms = lax.rsqrt(jnp.mean(h * h, axis=1, keepdims=True) + epsilon)
    dots = jnp.zeros((2, 1), F32)
    for b in range(NV):
        normed = h[:, b * CB:(b + 1) * CB] * inv_rms
        dots = dots + jnp.sum(rq[b] * gain[b] * normed, axis=1, keepdims=True)
    dots = dots / D
    for b in range(NV):
        normed = h[:, b * CB:(b + 1) * CB] * inv_rms
        gh_out[:, b * CB:(b + 1) * CB] = (inv_rms * (rq[b] * gain[b] - normed * dots)).astype(BF16)

    for copy in out_copies[NV - 2:]:
        copy.wait()
    for copy in pending:
        copy.wait_send()
    for o in (1, 3, 2):
        x_copy(o, x).wait_send()
    loop(NV - 1, lambda k: block_copy(k + 1).wait_send())
    loop(NZ - 1, lambda k: z_copy(k + 1).wait_send())
    loop(NZ - 1, lambda k: zr_copy(k + 1).wait_send())
    loop(NS - 1, lambda k: teach_copy(k + 1).wait_send())
    for flush in flushes:
        flush()


def shards(hidden, norm_gain, head_weight, teacher_logits, teacher_slot, valid_tokens):
    vmem = pl.BlockSpec(memory_space=pltpu.VMEM)
    hbm = pl.BlockSpec(memory_space=pl.ANY)
    scratch = [
        pltpu.VMEM((NY, NC, NJ, 128, COLS), BF16),
        pltpu.VMEM((NV, NZ, NX, 16, CB), BF16),
        pltpu.VMEM((NV, 2, CB), F32),
        pltpu.VMEM((NV, 2, CB), F32),
        pltpu.VMEM((16, CB), F32),
        pltpu.VMEM((4, 1024, 128), F32),
        pltpu.VMEM((NS, 32, COLS), BF16),
        pltpu.VMEM((NS, 32, COLS), BF16),
        pltpu.VMEM((ROWS, 1024), BF16),
        pltpu.VMEM((ROWS, COLS), F32),
        pltpu.VMEM((ROWS, COLS), F32),
        pltpu.VMEM((ROWS, 128), F32),
        pltpu.VMEM((NV, 8, ROWS), F32),
        pltpu.VMEM((NX, 8, ROWS), F32),
        pltpu.VMEM((NZ, 8, ROWS), F32),
        pltpu.VMEM((ROWS, COLS), BF16),
        pltpu.VMEM((NJ, NY, NZ, NX, 16, 128), F32),
        pltpu.VMEM((NJ, NY, NZ, NX, 16, 128), F32),
        pltpu.VMEM((NJ, NY, NZ, NX, 16, 128), F32),
        pltpu.VMEM((2, 2, 2, NZ, 16, 128), F32),
        pltpu.VMEM((2, 2, 2, 2, NZ, 16, 128), F32),
        pltpu.VMEM((2, 2, 4, NX, 16, 128), F32),
        pltpu.VMEM((2, 2, 2, 4, NX, 16, 128), F32),
        pltpu.VMEM((NZ, NY, NX, 16, 128), F32),
        pltpu.VMEM((2, NY, NZ, 16, 128), F32),
        pltpu.VMEM((2, NZ, NX, 16, 128), F32),
        pltpu.VMEM((NY, NX, 16, 128), F32),
        pltpu.VMEM((4, 2, 4, 16, 128), F32),
        pltpu.VMEM((4, 2, 2, 4, 16, 128), F32),
        pltpu.VMEM((2, 2, 16, 128), F32),
        pltpu.VMEM((2, 2, 2, 16, 128), F32),
        pltpu.VMEM((4, NZ, 16, 128), F32),
        pltpu.VMEM((4, NZ, 16, 128), F32),
        pltpu.VMEM((NY, 16, 128), F32),
        pltpu.VMEM((NY, 16, 128), F32),
        pltpu.VMEM((16, CB), F32),
        pltpu.VMEM((NV, 2, CB), F32),
        pltpu.VMEM((NV, 2, CB), F32),
        pltpu.VMEM((2, CB, COLS), BF16),
        pltpu.SemaphoreType.DMA((N_SEM,)),
        pltpu.SemaphoreType.DMA((N_SEM,)),
        pltpu.SemaphoreType.DMA,
        pltpu.SemaphoreType.DMA((2,)),
    ]
    grad_hidden, grad_head = pl.pallas_call(
        kernel,
        out_shape=(jax.ShapeDtypeStruct((2, D), BF16), jax.ShapeDtypeStruct((NV, CB, COLS), BF16)),
        in_specs=[vmem, vmem, vmem, vmem, hbm, vmem],
        out_specs=(vmem, hbm),
        scratch_shapes=scratch,
        compiler_params=pltpu.CompilerParams(
            collective_id=0, has_side_effects=True, vmem_limit_bytes=60 * 2**20
        ),
        name="distill_head",
    )(
        hidden,
        norm_gain.reshape(NV, 1, CB),
        teacher_slot.reshape(1, ROWS),
        valid_tokens.reshape(1, ROWS),
        head_weight.reshape(NY, NC, NJ, 128, COLS),
        teacher_logits.reshape(1024, COLS),
    )
    return grad_hidden, grad_head.reshape(D, COLS)


def solution(mesh):
    placed = (
        P(("seq", "vocab"), None),
        P(),
        P(None, ("seq", "vocab")),
        P("seq", None, "vocab"),
        P(),
        P(),
    )
    return jax.shard_map(
        shards,
        mesh=mesh,
        in_specs=placed,
        out_specs=(P(("seq", "vocab"), None), P(None, ("seq", "vocab"))),
        check_vma=False,
    )
```

time: 600 us -> 133 us (0.22)
  waiting for transfers between devices: 377 us -> 0 us
  blocking collectives: 148 us -> 0 us
  Pallas kernels: 0 us -> 126 us
  matrix products: 22.4 us -> 0 us
  between operations: 14.1 us -> 0.64 us
  starting transfers between devices: 11.9 us -> 0 us
  local copies, waits for them, and re-layouts: 16.4 us -> 6.53 us
  other arithmetic: 8.17 us -> 0 us
    unnamed x3 -> x0, waiting for transfers between devices: 271 us -> none
    pallas_call x0 -> x1, Pallas kernels: none -> 126 us  [shards(): pl.pallas_call(kernel, out_shape=(jax.ShapeDtypeStruct((2, D), BF16), jax...]
    all_gather x1 -> x0, waiting for transfers between devices: 81.7 us -> none  [shards(): gathered = lax.all_gather(features, ('seq', 'vocab'), axis=0, tiled=True)]
    pmax x1 -> x0, blocking collectives: 75.1 us -> none  [shards(): lax.pmax((jnp.max(logits, axis=1), jnp.max(teacher, axis=1)), ('seq', 'vo...]
    psum x1 -> x0, blocking collectives: 73.1 us -> none  [shards(): lax.psum((jnp.sum(shifted, axis=1), jnp.sum(shifted * (logits - teacher),...]
    all_to_all x1 -> x0, waiting for transfers between devices: 24.3 us -> none  [shards(): lax.all_to_all(teacher_logits, 'seq', split_axis=1, concat_axis=0, tiled=...]
    dot_general x3 -> x0, matrix products: 22.4 us -> none  [the longest x1 7.95 us: shards(): lax.dot_general(logit_grad, head_weight, (((1,), (1,)), ((), ())), prefer...]
    all_to_all x1 -> x0, starting transfers between devices: 11.9 us -> none  [shards(): lax.all_to_all(teacher_logits, 'seq', split_axis=1, concat_axis=0, tiled=...]
  transfers between devices with their start and end apart: 3 -> 0, of which waited for: 3 -> 0; matrix products, arithmetic and copies ran while one was open for 2% -> 0% of each run, Pallas kernels for 0% -> 0%
where the time goes in v1:
time: 133 us
  Pallas kernels  126 us (95%)
  local copies, waits for them, and re-layouts  6.53 us (5%)
    pallas_call x1, Pallas kernels, shards(): pl.pallas_call(kernel, out_shape=(jax.ShapeDtypeStruct((2, D), BF16), jax...  126 us
    unnamed x2, local copies, waits for them, and re-layouts  6.53 us

profile of v1, /device:TPU:1, one launch (start us, length us, event | category | flops | bytes accessed | tf_op | source)
XLA Modules:
  0.0 132.7 jit_solution(12333853512094345763)
XLA Ops:
  0.6 125.5 %distill_head.1 = (bf16[2,5120]{1,0:T(2,128)(2,1)}, bf16[8,640,512]{2,1,0:T(8,128)(2,1)}) custom-call(bf16[2,5120]{1,0:T(2,128)(2,1)} %hid.1, f32[8,1,640]{2,1,0:T(1,128)} %bitcast.9, s32[1,512]{1,0:T(1,128)} %bitcast.10, s32[1,512]{1,0:T(1,128)} %bitcast.11, bf16[4,2,5,128,512]{4,3,2,1,0:T(8,128)(2,1)} %bitcast.6, bf16[1024,512]{1,0:T(8,128)(2,1)} %bitcast.8), custom_call_target="tpu_custom_call" | custom-call | tf_op jit(solution)/shard_map/distill_head/pallas_call | solution.py:541
  126.2 1.3 %copy.10 = bf16[2,5120]{1,0:T(2,128)(2,1)} copy(bf16[2,5120]{1,0:T(2,128)(2,1)} %get-tuple-element.8) | data formatting | bytes 40960
  127.5 5.2 %copy.11 = bf16[5120,512]{1,0:T(8,128)(2,1)} copy(bf16[5120,512]{1,0:T(8,128)(2,1)} %bitcast.7) | data formatting | bytes 10485760

commit v2 on v1

v2 whole, which is shorter than its diff:
```python
import functools

import jax
import jax.numpy as jnp
from jax import lax
from jax.experimental import pallas as pl
from jax.experimental.pallas import tpu as pltpu
from jax.sharding import PartitionSpec as P

MESH = pl.DeviceIdType.MESH
F32 = jnp.float32
BF16 = jnp.bfloat16
epsilon = 1e-06

NZ, NX, NY, NC = 8, 4, 4, 2
NV, NS = NY * NC, NZ * NX
ROWS, D, CB, SB, COLS = 512, 5120, 640, 1024, 512
HALF = ROWS // NC
NJ = 5
ORDER = (4, 0, 2, 1, 3)
XFIRST, YFIRST = (0, 1), (2, 3)
N_SEM = 240
EARLY = 4
SPLIT = 5


class Links:
    def __init__(self, send, recv):
        self.send, self.recv, self.used = send, recv, 0

    def take(self, count=1):
        first = self.used
        self.used += count
        assert self.used <= N_SEM
        return first

    def copy(self, src, dst, device, index=None):
        if index is None:
            index = self.take()
        return pltpu.make_async_remote_copy(
            src_ref=src,
            dst_ref=dst,
            send_sem=self.send.at[index],
            recv_sem=self.recv.at[index],
            device_id=device,
            device_id_type=MESH,
        )


def mod(value, n):
    return lax.rem(value, n)


def loop(count, body):
    def step(i, carry):
        body(i)
        return carry

    lax.fori_loop(0, count, step, 0)


def kernel(
    hid, gain, slot, valid, w_hbm, teach_hbm,
    f_out, grad_out, rows_out,
    w, teach, f, ft, sf, zin, z32, t32, ts, tt, natural, column, onehot, logits, trow, st, sa, sb, sc, grad,
    po, ps, cr, poz, psz, crz, tx, rx, ty, ry, tza, tzb, rz, ax, ay, az, t2, r2, tz2, rz2, a2, zz, a2z, yy,
    send, recv, wsem, tsem, osem, relayed,
):
    s = lax.axis_index("seq")
    v = lax.axis_index("vocab")
    z, x = lax.div(s, NX), mod(s, NX)
    y, c = lax.div(v, NC), mod(v, NC)
    links = Links(send, recv)

    def at_s(other):
        return (other, v)

    def at_v(other):
        return (s, other)

    def at_z(other):
        return (other * NX + x, v)

    def at_x(other):
        return (z * NX + other, v)

    def at_y(other):
        return (s, other * NC + c)

    wcopy = pltpu.make_async_copy(w_hbm, w, wsem)
    tcopy = pltpu.make_async_copy(teach_hbm, teach, tsem)
    tcopy.start()
    barrier = pltpu.get_barrier_semaphore()

    def greet_vocab(k):
        pl.semaphore_signal(barrier, inc=1, device_id=at_v(mod(v + k + 1, NV)), device_id_type=MESH)

    def greet_z(k):
        pl.semaphore_signal(barrier, inc=1, device_id=at_z(mod(z + k + 1, NZ)), device_id_type=MESH)

    def greet_x(k):
        pl.semaphore_signal(barrier, inc=1, device_id=at_x(mod(x + k + 1, NX)), device_id_type=MESH)

    loop(NX - 1, greet_x)
    loop(NZ - 1, greet_z)
    loop(NV - 1, greet_vocab)
    wcopy.start()

    h = hid[...].astype(F32)
    inv_rms = lax.rsqrt(jnp.mean(h * h, axis=1, keepdims=True) + epsilon)
    for b in range(NV):
        part = h[:, b * CB:(b + 1) * CB] * inv_rms * gain[:, b * CB:(b + 1) * CB]
        for i in range(2):
            sf[i * NV + b:i * NV + b + 1, :] = part[i:i + 1, :]
    zin[z] = sf[...].astype(BF16)
    pl.semaphore_wait(barrier, NX - 1 + NZ - 1 + NV - 1)

    z_first = links.take(NZ)
    teach_first = links.take(NS)

    def z_copy(k):
        return links.copy(zin.at[z], zin.at[z], at_z(mod(z + k, NZ)), z_first + k)

    def z_arrival(k):
        source = mod(z + NZ - k, NZ)
        return links.copy(zin.at[source], zin.at[source], at_z(source), z_first + k)

    def z_pair(i):
        z_copy(4 - i).start()
        z_copy(4 + i).start()

    z_copy(4).start()
    loop(3, lambda i: z_pair(i + 1))

    def relay(k):
        pl.semaphore_signal(relayed, inc=1, device_id=at_x(mod(x + k + 1, NX)), device_id_type=MESH)

    loop(NX - 1, relay)

    def teach_copy(k):
        to = mod(s + k, NS)
        return links.copy(ts.at[to], tt.at[s], at_s(to), teach_first + k)

    def teach_arrival(k):
        source = mod(s + NS - k, NS)
        return links.copy(ts.at[source], tt.at[source], at_s(source), teach_first + k)

    def teach_pair(i):
        teach_copy(i + 1).start()
        teach_copy(NS - 1 - i).start()

    tcopy.wait()
    for b in range(4):
        t32[b] = teach[:, b * 128:(b + 1) * 128].astype(F32)

    def arrange(d):
        for b in range(4):
            ts[d, :, b * 128:(b + 1) * 128] = t32[b, pl.ds(d, 32, stride=NS), :].astype(BF16)

    loop(NS, arrange)
    tt[s] = ts[s]
    pl.semaphore_wait(relayed, NX - 1)
    loop(15, teach_pair)
    teach_copy(NS // 2).start()

    loop(NZ - 1, lambda k: z_arrival(k + 1).wait_recv())
    for b in range(CB // 128):
        z32[b] = zin[:, :, b * 128:(b + 1) * 128].astype(F32).reshape(NZ * 16, 128)
    for b in range(NV):
        for k in range(CB // 128):
            f[c, y, b, x, :, k * 128:(k + 1) * 128] = z32[k, pl.ds(b, 16, stride=NV), :].astype(BF16)

    offsets = (0, 1, 3, 2)
    other_core = (s, y * NC + (1 - c))
    pending, flushes = [], []

    def go(copy):
        copy.start()
        pending.append(copy)

    class Path:
        def __init__(self, span, x_last):
            self.span, self.x_last = span, x_last
            self.cut = (span[0] + span[1] + 1) // 2
            self.a, self.b = (y, x) if x_last else (x, y)
            self.to_a, self.to_b = (at_y, at_x) if x_last else (at_x, at_y)
            self.parts = [mod(self.a + 4 - o, 4) for o in offsets]
            self.up, self.down, self.far = mod(self.b + 1, 4), mod(self.b + 3, 4), mod(self.b + 2, 4)
            self.a_first, self.b_first, self.core_first = links.take(4), links.take(16), links.take(4)

        def ref(self, a, b, low=None, high=None):
            ya, xa = (a, b) if self.x_last else (b, a)
            low = self.span[0] if low is None else low
            high = self.span[1] if high is None else high
            return f.at[c, ya, low:high, xa]

        def a_copy(self, o, part):
            ref = self.ref(part, self.b)
            return links.copy(ref, ref, self.to_a(mod(self.a + o, 4)), self.a_first + o)

        def b_copy(self, kind, i, b, to, low=None, high=None):
            ref = self.ref(self.parts[i], b, low, high)
            return links.copy(ref, ref, self.to_b(to), self.b_first + kind * 4 + i)

        def own(self, i):
            go(self.b_copy(0, i, self.b, self.up))
            go(self.b_copy(1, i, self.b, self.down))

        def forward(self, i):
            self.b_copy(0, i, self.down, self.up).wait_recv()
            go(self.b_copy(2, i, self.down, self.up, None, self.cut))
            self.b_copy(1, i, self.up, self.down).wait_recv()
            go(self.b_copy(3, i, self.up, self.down, self.cut, None))

        def last(self, i):
            self.b_copy(2, i, self.far, self.up, None, self.cut).wait_recv()
            self.b_copy(3, i, self.far, self.down, self.cut, None).wait_recv()

        def core(self, rank, mine):
            b = (self.b, self.down, self.up, self.far)[rank]
            k = c if mine else 1 - c
            low, high = self.span
            ref = f.at[k, :, low:high, b] if self.x_last else f.at[k, b, low:high]
            return links.copy(ref, ref, other_core, self.core_first + rank)

    paths = (Path((0, SPLIT), False), Path((SPLIT, NV), True))
    for path in paths:
        for o in (1, 3, 2):
            go(path.a_copy(o, path.a))
    for path in paths:
        path.own(0)

    quantity = lax.broadcasted_iota(jnp.int32, (128, ROWS), 0)
    natural[...] = jnp.where(quantity == 0, slot[...].astype(F32), valid[...].astype(F32)).T
    for k in range(NC * NY * NX * 2):
        kc, ky, kx, ki = k // 32, k // 8 % 4, k // 2 % 4, k % 2
        column[pl.ds(kc * 256 + ky * 64 + kx * 16 + ki, NZ, stride=2), :] = natural[
            pl.ds(kx * 16 + ky * 4 + kc * 2 + ki, NZ, stride=64), :]

    lane = lax.broadcasted_iota(jnp.int32, (ROWS, 128), 1).astype(F32)
    for b in range(8):
        onehot[:, b * 128:(b + 1) * 128] = jnp.where(column[:, 0:1] == lane + float(b * 128), 1.0, 0.0).astype(BF16)

    for i, o in enumerate(offsets):
        if o:
            for path in paths:
                path.a_copy(o, path.parts[i]).wait_recv()
                path.own(i)
    for path in paths:
        go(path.core(0, True))
    for i in range(4):
        for path in paths:
            path.forward(i)
    for path in paths:
        go(path.core(1, True))
        go(path.core(2, True))
    wcopy.wait()

    def multiply(half):
        logits[half] = jnp.zeros((HALF, COLS), F32)

        def block(b):
            fb = f[half, :, b].reshape(HALF, CB)
            wb = w[pl.ds(b * 5, 5)].reshape(CB, COLS)
            logits[half] += jnp.dot(fb, wb, preferred_element_type=F32)

        loop(NV, block)

    for path in paths:
        for i in range(4):
            path.last(i)
        go(path.core(3, True))
    multiply(c)
    for path in paths:
        for rank in range(4):
            path.core(rank, False).wait_recv()
    multiply(1 - c)

    loop(NS - 1, lambda k: teach_arrival(k + 1).wait_recv())

    def select(i):
        span = pl.ds(pl.multiple_of(i * 256, 256), 256)
        trow[i] = jnp.dot(onehot[span, :], tt[...].reshape(1024, COLS), preferred_element_type=F32)

    loop(2, select)

    def statistics(i):
        span = pl.ds(pl.multiple_of(i * 64, 64), 64)
        inner = pl.ds(pl.multiple_of(mod(i, 4) * 64, 64), 64)
        lo, te = logits[lax.div(i, 4), inner, :], trow[lax.div(i, 4), inner, :]
        top = jnp.max(lo, axis=1, keepdims=True)
        teacher_top = jnp.max(te, axis=1, keepdims=True)
        e = jnp.exp(lo - top)
        total = jnp.sum(e, axis=1, keepdims=True)
        cross = jnp.sum(e * (lo - te), axis=1, keepdims=True)
        teacher_total = jnp.sum(jnp.exp(te - teacher_top), axis=1, keepdims=True)
        place = lax.broadcasted_iota(jnp.int32, (64, 128), 1)
        packed = jnp.where(place == 0, top, jnp.where(place == 1, teacher_top, jnp.where(place == 2, total, jnp.where(
            place == 3, cross, jnp.where(place == 4, teacher_total, 0.0)))))
        st[span, :] = packed

    loop(8, statistics)

    def merged(ref):
        value = ref[...]
        top = jnp.max(value[:, 0:1, :], axis=0, keepdims=True)
        teacher_top = jnp.max(value[:, 1:2, :], axis=0, keepdims=True)
        scale = jnp.exp(value[:, 0:1, :] - top)
        teacher_scale = jnp.exp(value[:, 1:2, :] - teacher_top)
        total = jnp.sum(value[:, 2:3, :] * scale, axis=0)
        cross = jnp.sum(value[:, 3:4, :] * scale, axis=0)
        teacher_total = jnp.sum(value[:, 4:5, :] * teacher_scale, axis=0)
        return top[0], teacher_top[0], total, cross, teacher_total

    def exchange(buffer, here, count, device, blocks):
        start = links.take(count)

        def out(k):
            return links.copy(buffer.at[here], buffer.at[here], device(mod(here + k, count)), start + k)

        def arrival(k):
            source = mod(here + count - k, count)
            return links.copy(buffer.at[source], buffer.at[source], device(source), start + k)

        loop(count - 1, lambda k: out(k + 1).start())
        for b in blocks:
            ft[b] = f[:, :, b].reshape(ROWS, CB).T
        loop(count - 1, lambda k: arrival(k + 1).wait_recv())
        return lambda: loop(count - 1, lambda k: out(k + 1).wait_send())

    def put(buffer, here, rows):
        for r, row in enumerate(rows):
            buffer[here, r:r + 1, :] = row

    sa[v] = st[...].T[0:8, :]
    flushes.append(exchange(sa, v, NV, at_v, (0, 1, 2)))
    put(sb, x, merged(sa))
    flushes.append(exchange(sb, x, NX, at_x, (3, 4)))
    put(sc, z, merged(sb))
    flushes.append(exchange(sc, z, NZ, at_z, (5, 6, 7)))
    f_copy = pltpu.make_async_copy(ft, f_out, osem.at[0])
    f_copy.start()
    top, teacher_top, total, cross, teacher_total = merged(sc)
    student_lse = top + jnp.log(total)
    teacher_lse = teacher_top + jnp.log(teacher_total)
    divergence = cross / total - student_lse + teacher_lse
    st[...] = jnp.where(quantity == 0, student_lse, jnp.where(quantity == 1, teacher_lse, jnp.where(
        quantity == 2, divergence, 0.0))).T

    def gradient(i):
        span = pl.ds(pl.multiple_of(i * 64, 64), 64)
        inner = pl.ds(pl.multiple_of(mod(i, 4) * 64, 64), 64)
        lo, te, q = logits[lax.div(i, 4), inner, :], trow[lax.div(i, 4), inner, :], st[span, :]
        shifted = lo - q[:, 0:1]
        gap = shifted - (te - q[:, 1:2])
        grad[span, :] = (column[span, 1:2] * jnp.exp(shifted) * (gap - q[:, 2:3])).astype(BF16)

    loop(8, gradient)
    grad_copy = pltpu.make_async_copy(grad, grad_out, osem.at[1])
    grad_copy.start()

    def partial(j, half, ref):
        g = grad[pl.ds(pl.multiple_of(half * HALF, HALF), HALF), :]
        if j == 4:
            at = lax.broadcasted_iota(jnp.int32, (HALF, HALF), 0)
            source = (at // 2 % 4) * 64 + (at // 8 % 4) * 16 + (at // 32) * 2 + at % 2
            move = jnp.where(source == lax.broadcasted_iota(jnp.int32, (HALF, HALF), 1), 1.0, 0.0).astype(BF16)
            g = jnp.dot(move, g, preferred_element_type=F32).astype(BF16)
        for n in range(2):
            wn = w[j * 8 + n * 4:j * 8 + n * 4 + 4].reshape(512, COLS)
            product = lax.dot_general(g, wn, (((1,), (1,)), ((), ())), preferred_element_type=F32)
            if j == 4:
                ref[:, :, :, n * 512:(n + 1) * 512] = product.reshape(NZ, NX, 8, 512)
            else:
                ref[j, :, :, :, n * 512:(n + 1) * 512] = product.reshape(NY, NX, 16, 512)

    def add_core(j):
        def step(i):
            if j == 4:
                psz[i] += crz[i]
            else:
                ps[j, i] += cr[j, i]

        loop(NZ if j == 4 else NY, step)

    class Ring:
        def __init__(self, here, device, block, tmp, arrived):
            self.block, self.tmp, self.arrived, self.here = block, tmp, arrived, here
            up, down, far = mod(here + 1, 4), mod(here + 3, 4), mod(here + 2, 4)
            self.up, self.down = up, down
            self.far0 = links.copy(block(far, 0), tmp.at[0], device(up))
            self.far1 = links.copy(block(far, 1), tmp.at[1], device(down))
            self.free0 = links.copy(block(up, 1), arrived.at[0, 1], device(up))
            self.free1 = links.copy(block(down, 0), arrived.at[1, 0], device(down))
            self.last0 = links.copy(tmp.at[0], arrived.at[0, 0], device(up))
            self.last1 = links.copy(tmp.at[1], arrived.at[1, 1], device(down))
            for copy in (self.far0, self.far1, self.free0, self.free1):
                go(copy)

        def middle(self):
            self.far0.wait_recv()
            self.tmp[0] = self.tmp[0] + self.block(self.up, 0)[...]
            go(self.last0)
            self.far1.wait_recv()
            self.tmp[1] = self.tmp[1] + self.block(self.down, 1)[...]
            go(self.last1)

        def finish(self):
            for copy in (self.free0, self.free1, self.last0, self.last1):
                copy.wait_recv()
            return [self.block(self.here, i)[...] + self.arrived[0, i] + self.arrived[1, i] for i in (0, 1)]

    core_links = {j: links.copy(poz, crz, other_core) if j == 4 else links.copy(po.at[j], cr.at[j], other_core) for j in ORDER}
    stage1 = {}

    class Line:
        def __init__(self):
            p = [mod(z + k, NZ) for k in range(NZ)]
            self.p = p
            self.near = [links.copy(psz.at[p[1]], rz.at[0], at_z(p[1])), links.copy(psz.at[p[7]], rz.at[1], at_z(p[7]))]
            self.far = [
                links.copy(psz.at[p[3]], tza.at[0], at_z(p[1])),
                links.copy(psz.at[p[5]], tza.at[1], at_z(p[7])),
                links.copy(psz.at[p[4], 0:2], tzb.at[0], at_z(p[2])),
                links.copy(psz.at[p[4], 2:4], tzb.at[1], at_z(p[6])),
            ]
            self.summed = [links.copy(tza.at[0], rz.at[2], at_z(p[2])), links.copy(tza.at[1], rz.at[3], at_z(p[6]))]
            for copy in self.far + self.near:
                go(copy)

        def middle(self):
            for i, k in ((0, 2), (1, 6)):
                self.far[i].wait_recv()
                self.far[i + 2].wait_recv()
                tza[i] += psz[self.p[k]]
                tza[i, 2 * i:2 * i + 2] += tzb[i]
                go(self.summed[i])

        def finish(self):
            for copy in self.near + self.summed:
                copy.wait_recv()
            az[...] = psz[z] + rz[0] + rz[1] + rz[2] + rz[3]

    def begin(j):
        core_links[j].wait_recv()
        add_core(j)
        if j in XFIRST:
            stage1[j] = Ring(x, at_x, lambda i, half, j=j: ps.at[j, half * 2:half * 2 + 2, i], tx.at[j], rx.at[j])
        elif j in YFIRST:
            stage1[j] = Ring(y, at_y, lambda i, half, j=j: ps.at[j, i, half * 2:half * 2 + 2], ty.at[j - 2], ry.at[j - 2])
        else:
            stage1[j] = Line()

    for n, j in enumerate(ORDER):
        partial(j, 1 - c, poz if j == 4 else po)
        go(core_links[j])
        partial(j, c, psz if j == 4 else ps)
        if n:
            begin(ORDER[n - 1])
    begin(ORDER[-1])

    for j in (0, 2, 4, 1, 3):
        stage1[j].middle()

    def spread(buffer, source, here, count, device):
        start = links.take(count)

        def out(k):
            to = mod(here + k, count)
            return links.copy(source.at[to], buffer.at[here], device(to), start + k)

        def arrival(k):
            other = mod(here + count - k, count)
            return links.copy(source.at[other], buffer.at[other], device(other), start + k)

        loop(count - 1, lambda k: out(k + 1).start())
        buffer[here] = source[here]
        flushes.append(lambda: loop(count - 1, lambda k: out(k + 1).wait_send()))
        return lambda: loop(count - 1, lambda k: arrival(k + 1).wait_recv())

    stage2, stage3 = {}, {}
    for j in (0, 2, 1, 3, 4):
        if j == 4:
            stage1[4].finish()
            stage2[4] = Ring(x, at_x, lambda i, half: az.at[i, :, half * 512:half * 512 + 512], tz2, rz2)
            continue
        low, high = stage1[j].finish()
        mine = ax.at[j] if j in XFIRST else ay.at[j - 2]
        mine[0:2] = low
        mine[2:4] = high
        here, device = (y, at_y) if j in XFIRST else (x, at_x)
        stage2[j] = Ring(here, device, lambda i, half, m=mine: m.at[i, half * 8:half * 8 + 8], t2.at[j], r2.at[j])
    for j in (0, 2, 1, 3, 4):
        stage2[j].middle()
    for j in (0, 2, 1, 3, 4):
        low, high = stage2[j].finish()
        if j == 4:
            for k in range(NY):
                a2z[k, :, 0:512] = low[2 * k:2 * k + 2, :]
                a2z[k, :, 512:1024] = high[2 * k:2 * k + 2, :]
            stage3[j] = spread(yy, a2z, y, NY, at_y)
        else:
            for k in range(4):
                a2[j, k] = low[2 * k:2 * k + 2, :]
                a2[j, k + 4] = high[2 * k:2 * k + 2, :]
            stage3[j] = spread(zz.at[j], a2.at[j], z, NZ, at_z)
    for j in (0, 2, 1, 3, 4):
        stage3[j]()
        arrived = yy[...] if j == 4 else zz[j]
        rows_out[j] = jnp.sum(arrived, axis=0)

    f_copy.wait()
    grad_copy.wait()
    for copy in pending:
        copy.wait_send()
    loop(NZ - 1, lambda k: z_copy(k + 1).wait_send())
    loop(NS - 1, lambda k: teach_copy(k + 1).wait_send())
    for flush in flushes:
        flush()


def finish_kernel(hid, gain, rows, f_hbm, grad_hbm, gh_out, head_hbm, f, grad, stage, gsem, fsem, osem):
    gcopy = pltpu.make_async_copy(grad_hbm, grad, gsem)
    gcopy.start()
    fcopies = [pltpu.make_async_copy(f_hbm.at[b], f.at[b], fsem.at[b]) for b in range(NV)]
    ocopies = [pltpu.make_async_copy(stage.at[b], head_hbm.at[b], osem.at[b]) for b in range(NV)]
    for copy in fcopies:
        copy.start()
    h = hid[...].astype(F32)
    inv_rms = lax.rsqrt(jnp.mean(h * h, axis=1, keepdims=True) + epsilon)
    dots = jnp.zeros((2, 1), F32)
    for j in range(NJ):
        span = slice(j * SB, (j + 1) * SB)
        dots = dots + jnp.sum(rows[j] * gain[:, span] * (h[:, span] * inv_rms), axis=1, keepdims=True)
    dots = dots / D
    for j in range(NJ):
        span = slice(j * SB, (j + 1) * SB)
        gh_out[:, span] = (inv_rms * (rows[j] * gain[:, span] - h[:, span] * inv_rms * dots)).astype(BF16)
    gcopy.wait()
    for b in range(NV):
        fcopies[b].wait()
        stage[b] = jnp.dot(f[b], grad[...], preferred_element_type=F32).astype(BF16)
        ocopies[b].start()
    for copy in ocopies:
        copy.wait()


def shards(hidden, norm_gain, head_weight, teacher_logits, teacher_slot, valid_tokens):
    vmem = pl.BlockSpec(memory_space=pltpu.VMEM)
    hbm = pl.BlockSpec(memory_space=pl.ANY)
    scratch = [
        pltpu.VMEM((40, 128, COLS), BF16),
        pltpu.VMEM((1024, COLS), BF16),
        pltpu.VMEM((NC, NY, NV, NX, 16, CB), BF16),
        pltpu.VMEM((NV, CB, ROWS), BF16),
        pltpu.VMEM((16, CB), F32),
        pltpu.VMEM((NZ, 16, CB), BF16),
        pltpu.VMEM((5, 128, 128), F32),
        pltpu.VMEM((4, 1024, 128), F32),
        pltpu.VMEM((NS, 32, COLS), BF16),
        pltpu.VMEM((NS, 32, COLS), BF16),
        pltpu.VMEM((ROWS, 128), F32),
        pltpu.VMEM((ROWS, 128), F32),
        pltpu.VMEM((ROWS, 1024), BF16),
        pltpu.VMEM((NC, HALF, COLS), F32),
        pltpu.VMEM((NC, HALF, COLS), F32),
        pltpu.VMEM((ROWS, 128), F32),
        pltpu.VMEM((NV, 8, ROWS), F32),
        pltpu.VMEM((NX, 8, ROWS), F32),
        pltpu.VMEM((NZ, 8, ROWS), F32),
        pltpu.VMEM((ROWS, COLS), BF16),
        pltpu.VMEM((4, NY, NX, 16, SB), F32),
        pltpu.VMEM((4, NY, NX, 16, SB), F32),
        pltpu.VMEM((4, NY, NX, 16, SB), F32),
        pltpu.VMEM((NZ, NX, 8, SB), F32),
        pltpu.VMEM((NZ, NX, 8, SB), F32),
        pltpu.VMEM((NZ, NX, 8, SB), F32),
        pltpu.VMEM((2, 2, 2, 16, SB), F32),
        pltpu.VMEM((2, 2, 2, 2, 16, SB), F32),
        pltpu.VMEM((2, 2, 2, 16, SB), F32),
        pltpu.VMEM((2, 2, 2, 2, 16, SB), F32),
        pltpu.VMEM((2, NX, 8, SB), F32),
        pltpu.VMEM((2, 2, 8, SB), F32),
        pltpu.VMEM((4, NX, 8, SB), F32),
        pltpu.VMEM((2, NY, 16, SB), F32),
        pltpu.VMEM((2, NX, 16, SB), F32),
        pltpu.VMEM((NX, 8, SB), F32),
        pltpu.VMEM((4, 2, 8, SB), F32),
        pltpu.VMEM((4, 2, 2, 8, SB), F32),
        pltpu.VMEM((2, 8, SB // 2), F32),
        pltpu.VMEM((2, 2, 8, SB // 2), F32),
        pltpu.VMEM((4, NZ, 2, SB), F32),
        pltpu.VMEM((4, NZ, 2, SB), F32),
        pltpu.VMEM((NY, 2, SB), F32),
        pltpu.VMEM((NY, 2, SB), F32),
        pltpu.SemaphoreType.DMA((N_SEM,)),
        pltpu.SemaphoreType.DMA((N_SEM,)),
        pltpu.SemaphoreType.DMA,
        pltpu.SemaphoreType.DMA,
        pltpu.SemaphoreType.DMA((2,)),
        pltpu.SemaphoreType.REGULAR,
    ]
    gain = norm_gain.reshape(1, D)
    features, grad, rows = pl.pallas_call(
        kernel,
        out_shape=(
            jax.ShapeDtypeStruct((NV, CB, ROWS), BF16),
            jax.ShapeDtypeStruct((ROWS, COLS), BF16),
            jax.ShapeDtypeStruct((NJ, 2, SB), F32),
        ),
        in_specs=[vmem, vmem, vmem, vmem, hbm, hbm],
        out_specs=(hbm, hbm, vmem),
        scratch_shapes=scratch,
        compiler_params=pltpu.CompilerParams(
            collective_id=0, has_side_effects=True, vmem_limit_bytes=60 * 2**20
        ),
        name="distill_head",
    )(
        hidden,
        gain,
        teacher_slot.reshape(1, ROWS),
        valid_tokens.reshape(1, ROWS),
        head_weight.reshape(40, 128, COLS),
        teacher_logits.reshape(1024, COLS),
    )

    grad_hidden, grad_head = pl.pallas_call(
        finish_kernel,
        out_shape=(jax.ShapeDtypeStruct((2, D), BF16), jax.ShapeDtypeStruct((NV, CB, COLS), BF16)),
        in_specs=[vmem, vmem, vmem, hbm, hbm],
        out_specs=(vmem, hbm),
        scratch_shapes=[
            pltpu.VMEM((NV, CB, ROWS), BF16),
            pltpu.VMEM((ROWS, COLS), BF16),
            pltpu.VMEM((NV, CB, COLS), BF16),
            pltpu.SemaphoreType.DMA,
            pltpu.SemaphoreType.DMA((NV,)),
            pltpu.SemaphoreType.DMA((NV,)),
        ],
        compiler_params=pltpu.CompilerParams(vmem_limit_bytes=60 * 2**20),
        name="head_gradient",
    )(hidden, gain, rows, features, grad)
    return grad_hidden, grad_head.reshape(D, COLS)


def solution(mesh):
    placed = (
        P(("seq", "vocab"), None),
        P(),
        P(None, ("seq", "vocab")),
        P("seq", None, "vocab"),
        P(),
        P(),
    )
    return jax.shard_map(
        shards,
        mesh=mesh,
        in_specs=placed,
        out_specs=(P(("seq", "vocab"), None), P(None, ("seq", "vocab"))),
        check_vma=False,
    )
```

time: 133 us -> 116 us (0.87)
  Pallas kernels: 126 us -> 115 us
  local copies, waits for them, and re-layouts: 6.53 us -> 0 us
    pallas_call x1 -> x2, Pallas kernels: 126 us -> 115 us  [the longest x1 106 us: shards(): pl.pallas_call(kernel, out_shape=(jax.ShapeDtypeStruct((NV, CB, ROWS), BF...]
    unnamed x2 -> x0, local copies, waits for them, and re-layouts: 6.53 us -> none
where the time goes in v2:
time: 116 us; the launch traced here: 115 us
  Pallas kernels  115 us (99%)
    pallas_call x1, Pallas kernels, shards(): pl.pallas_call(kernel, out_shape=(jax.ShapeDtypeStruct((NV, CB, ROWS), BF...  106 us
    pallas_call x1, Pallas kernels, shards(): pl.pallas_call(finish_kernel, out_shape=(jax.ShapeDtypeStruct((2, D), BF1...  8.89 us

profile of v2, /device:TPU:1, one launch (start us, length us, event | category | flops | bytes accessed | tf_op | source)
XLA Modules:
  0.0 115.4 jit_solution(3092778386253770438)
XLA Ops:
  0.6 105.8 %distill_head.1 = (bf16[8,640,512]{2,1,0:T(8,128)(2,1)}, bf16[512,512]{1,0:T(8,128)(2,1)}, f32[5,2,1024]{2,1,0:T(2,128)}) custom-call(bf16[2,5120]{1,0:T(2,128)(2,1)} %hid.3, f32[1,5120]{1,0:T(1,128)} %bitcast.8, s32[1,512]{1,0:T(1,128)} %bitcast.10, s32[1,512]{1,0:T(1,128)} %bitcast.11, bf16[40,128,512]{2,1,0:T(8,128)(2,1)} %bitcast.6, ...), custom_call_target="tpu_custom_call" | custom-call | tf_op jit(solution)/shard_map/distill_head/pallas_call | solution.py:604
  106.5 8.9 %head_gradient.1 = (bf16[2,5120]{1,0:T(2,128)(2,1)}, bf16[8,640,512]{2,1,0:T(8,128)(2,1)}) custom-call(bf16[2,5120]{1,0:T(2,128)(2,1)} %hid.3, f32[1,5120]{1,0:T(1,128)} %bitcast.9, f32[5,2,1024]{2,1,0:T(2,128)} %get-tuple-element.7.rows, bf16[8,640,512]{2,1,0:T(8,128)(2,1)} %get-tuple-element.8.f_hbm, bf16[512,512]{1,0:T(8,128)(2,1)} %get-tuple-element.9.grad_hbm), custom_call_target="tpu_custom_call" | custom-call | tf_op jit(solution)/shard_map/head_gradient/pallas_call | solution.py:627

commit v3 on v2

--- a/solution.py
+++ b/solution.py
@@ -20,8 +20,9 @@
 ORDER = (4, 0, 2, 1, 3)
 XFIRST, YFIRST = (0, 1), (2, 3)
 N_SEM = 240
-EARLY = 4
-SPLIT = 5
+LIMIT = 55
+FIRST = 7
+SPLIT = 6
 
 
 class Links:
@@ -60,11 +61,11 @@
 
 
 def kernel(
-    hid, gain, slot, valid, w_hbm, teach_hbm,
-    f_out, grad_out, rows_out,
-    w, teach, f, ft, sf, zin, z32, t32, ts, tt, natural, column, onehot, logits, trow, st, sa, sb, sc, grad,
+    hid_hbm, gain_hbm, slot_hbm, valid_hbm, w_hbm, teach_hbm,
+    ft, grad, rows,
+    hid, gain, slot, valid, w, teach, f, sf, zin, z32, t32, ts, tt, natural, column, onehot, logits, trow, st, sa, sb, sc,
     po, ps, cr, poz, psz, crz, tx, rx, ty, ry, tza, tzb, rz, ax, ay, az, t2, r2, tz2, rz2, a2, zz, a2z, yy,
-    send, recv, wsem, tsem, osem, relayed,
+    send, recv, isem, wsem, tsem, relayed,
 ):
     s = lax.axis_index("seq")
     v = lax.axis_index("vocab")
@@ -89,6 +90,12 @@
 
     wcopy = pltpu.make_async_copy(w_hbm, w, wsem)
     tcopy = pltpu.make_async_copy(teach_hbm, teach, tsem)
+    inputs = [
+        pltpu.make_async_copy(source, target, isem.at[i])
+        for i, (source, target) in enumerate(((hid_hbm, hid), (gain_hbm, gain), (slot_hbm, slot), (valid_hbm, valid)))
+    ]
+    for copy in inputs:
+        copy.start()
     tcopy.start()
     barrier = pltpu.get_barrier_semaphore()
 
@@ -106,6 +113,8 @@
     loop(NV - 1, greet_vocab)
     wcopy.start()
 
+    for copy in inputs:
+        copy.wait()
     h = hid[...].astype(F32)
     inv_rms = lax.rsqrt(jnp.mean(h * h, axis=1, keepdims=True) + epsilon)
     for b in range(NV):
@@ -137,17 +146,15 @@
 
     loop(NX - 1, relay)
 
-    def teach_copy(k):
-        to = mod(s + k, NS)
-        return links.copy(ts.at[to], tt.at[s], at_s(to), teach_first + k)
-
-    def teach_arrival(k):
-        source = mod(s + NS - k, NS)
-        return links.copy(ts.at[source], tt.at[source], at_s(source), teach_first + k)
-
-    def teach_pair(i):
-        teach_copy(i + 1).start()
-        teach_copy(NS - 1 - i).start()
+    def teach_copy(dz, dx):
+        to = mod(z + dz, NZ) * NX + mod(x + dx, NX)
+        return links.copy(ts.at[to], tt.at[s], at_s(to), teach_first + dz * NX + dx)
+
+    def teach_arrival(dz, dx):
+        source = mod(z + NZ - dz, NZ) * NX + mod(x + NX - dx, NX)
+        return links.copy(ts.at[source], tt.at[source], at_s(source), teach_first + dz * NX + dx)
+
+    teach_order = [(dz, dx) for dx in (0, 1, 3, 2) for dz in (0, 1, 7, 2, 6, 3, 5, 4) if dz or dx]
 
     tcopy.wait()
     for b in range(4):
@@ -160,8 +167,8 @@
     loop(NS, arrange)
     tt[s] = ts[s]
     pl.semaphore_wait(relayed, NX - 1)
-    loop(15, teach_pair)
-    teach_copy(NS // 2).start()
+    for dz, dx in teach_order[:FIRST]:
+        teach_copy(dz, dx).start()
 
     loop(NZ - 1, lambda k: z_arrival(k + 1).wait_recv())
     for b in range(CB // 128):
@@ -229,6 +236,9 @@
             go(path.a_copy(o, path.a))
     for path in paths:
         path.own(0)
+
+    for dz, dx in teach_order[FIRST:]:
+        teach_copy(dz, dx).start()
 
     quantity = lax.broadcasted_iota(jnp.int32, (128, ROWS), 0)
     natural[...] = jnp.where(quantity == 0, slot[...].astype(F32), valid[...].astype(F32)).T
@@ -276,7 +286,8 @@
             path.core(rank, False).wait_recv()
     multiply(1 - c)
 
-    loop(NS - 1, lambda k: teach_arrival(k + 1).wait_recv())
+    for dz, dx in teach_order:
+        teach_arrival(dz, dx).wait_recv()
 
     def select(i):
         span = pl.ds(pl.multiple_of(i * 256, 256), 256)
@@ -295,22 +306,24 @@
         cross = jnp.sum(e * (lo - te), axis=1, keepdims=True)
         teacher_total = jnp.sum(jnp.exp(te - teacher_top), axis=1, keepdims=True)
         place = lax.broadcasted_iota(jnp.int32, (64, 128), 1)
-        packed = jnp.where(place == 0, top, jnp.where(place == 1, teacher_top, jnp.where(place == 2, total, jnp.where(
-            place == 3, cross, jnp.where(place == 4, teacher_total, 0.0)))))
+        packed = jnp.where(place == 0, top + jnp.log(total), jnp.where(
+            place == 1, teacher_top + jnp.log(teacher_total), jnp.where(place == 2, cross / total, 0.0)))
         st[span, :] = packed
 
     loop(8, statistics)
 
     def merged(ref):
         value = ref[...]
-        top = jnp.max(value[:, 0:1, :], axis=0, keepdims=True)
-        teacher_top = jnp.max(value[:, 1:2, :], axis=0, keepdims=True)
-        scale = jnp.exp(value[:, 0:1, :] - top)
-        teacher_scale = jnp.exp(value[:, 1:2, :] - teacher_top)
-        total = jnp.sum(value[:, 2:3, :] * scale, axis=0)
-        cross = jnp.sum(value[:, 3:4, :] * scale, axis=0)
-        teacher_total = jnp.sum(value[:, 4:5, :] * teacher_scale, axis=0)
-        return top[0], teacher_top[0], total, cross, teacher_total
+
+        def lse(part):
+            top = jnp.max(part, axis=0)
+            scale = jnp.exp(part - top[None])
+            total = jnp.sum(scale, axis=0)
+            return top + jnp.log(total), scale, total
+
+        student_lse, scale, total = lse(value[:, 0:1, :])
+        teacher_lse, _, _ = lse(value[:, 1:2, :])
+        return student_lse, teacher_lse, jnp.sum(scale * value[:, 2:3, :], axis=0) / total
 
     def exchange(buffer, here, count, device, blocks):
         start = links.take(count)
@@ -332,18 +345,14 @@
         for r, row in enumerate(rows):
             buffer[here, r:r + 1, :] = row
 
-    sa[v] = st[...].T[0:8, :]
+    sa[v] = st[...].T[0:4, :]
     flushes.append(exchange(sa, v, NV, at_v, (0, 1, 2)))
     put(sb, x, merged(sa))
     flushes.append(exchange(sb, x, NX, at_x, (3, 4)))
     put(sc, z, merged(sb))
     flushes.append(exchange(sc, z, NZ, at_z, (5, 6, 7)))
-    f_copy = pltpu.make_async_copy(ft, f_out, osem.at[0])
-    f_copy.start()
-    top, teacher_top, total, cross, teacher_total = merged(sc)
-    student_lse = top + jnp.log(total)
-    teacher_lse = teacher_top + jnp.log(teacher_total)
-    divergence = cross / total - student_lse + teacher_lse
+    student_lse, teacher_lse, mean_gap = merged(sc)
+    divergence = mean_gap - student_lse + teacher_lse
     st[...] = jnp.where(quantity == 0, student_lse, jnp.where(quantity == 1, teacher_lse, jnp.where(
         quantity == 2, divergence, 0.0))).T
 
@@ -356,8 +365,6 @@
         grad[span, :] = (column[span, 1:2] * jnp.exp(shifted) * (gap - q[:, 2:3])).astype(BF16)
 
     loop(8, gradient)
-    grad_copy = pltpu.make_async_copy(grad, grad_out, osem.at[1])
-    grad_copy.start()
 
     def partial(j, half, ref):
         g = grad[pl.ds(pl.multiple_of(half * HALF, HALF), HALF), :]
@@ -479,20 +486,20 @@
         return lambda: loop(count - 1, lambda k: arrival(k + 1).wait_recv())
 
     stage2, stage3 = {}, {}
-    for j in (0, 2, 1, 3, 4):
+
+    def second(j):
         if j == 4:
             stage1[4].finish()
             stage2[4] = Ring(x, at_x, lambda i, half: az.at[i, :, half * 512:half * 512 + 512], tz2, rz2)
-            continue
+            return
         low, high = stage1[j].finish()
         mine = ax.at[j] if j in XFIRST else ay.at[j - 2]
         mine[0:2] = low
         mine[2:4] = high
         here, device = (y, at_y) if j in XFIRST else (x, at_x)
-        stage2[j] = Ring(here, device, lambda i, half, m=mine: m.at[i, half * 8:half * 8 + 8], t2.at[j], r2.at[j])
-    for j in (0, 2, 1, 3, 4):
-        stage2[j].middle()
-    for j in (0, 2, 1, 3, 4):
+        stage2[j] = Ring(here, device, lambda i, half: mine.at[i, half * 8:half * 8 + 8], t2.at[j], r2.at[j])
+
+    def third(j):
         low, high = stage2[j].finish()
         if j == 4:
             for k in range(NY):
@@ -504,28 +511,41 @@
                 a2[j, k] = low[2 * k:2 * k + 2, :]
                 a2[j, k + 4] = high[2 * k:2 * k + 2, :]
             stage3[j] = spread(zz.at[j], a2.at[j], z, NZ, at_z)
+
+    for j in (0, 2, 1, 3, 4):
+        second(j)
+    for j in (0, 2, 1, 3, 4):
+        stage2[j].middle()
+    for j in (0, 2, 1, 3, 4):
+        third(j)
     for j in (0, 2, 1, 3, 4):
         stage3[j]()
-        arrived = yy[...] if j == 4 else zz[j]
-        rows_out[j] = jnp.sum(arrived, axis=0)
-
-    f_copy.wait()
-    grad_copy.wait()
+        rows[j] = jnp.sum(yy[...] if j == 4 else zz[j], axis=0)
+
     for copy in pending:
         copy.wait_send()
     loop(NZ - 1, lambda k: z_copy(k + 1).wait_send())
-    loop(NS - 1, lambda k: teach_copy(k + 1).wait_send())
+    for dz, dx in teach_order:
+        teach_copy(dz, dx).wait_send()
     for flush in flushes:
         flush()
 
 
-def finish_kernel(hid, gain, rows, f_hbm, grad_hbm, gh_out, head_hbm, f, grad, stage, gsem, fsem, osem):
-    gcopy = pltpu.make_async_copy(grad_hbm, grad, gsem)
-    gcopy.start()
-    fcopies = [pltpu.make_async_copy(f_hbm.at[b], f.at[b], fsem.at[b]) for b in range(NV)]
-    ocopies = [pltpu.make_async_copy(stage.at[b], head_hbm.at[b], osem.at[b]) for b in range(NV)]
-    for copy in fcopies:
+def finish_kernel(hid_hbm, gain_hbm, rows, ft, grad, gh_hbm, head_hbm, hid, gain, gh, stage, isem, osem):
+    inputs = [pltpu.make_async_copy(hid_hbm, hid, isem.at[0]), pltpu.make_async_copy(gain_hbm, gain, isem.at[1])]
+    outputs = [pltpu.make_async_copy(stage.at[b], head_hbm.at[b], osem.at[b]) for b in range(NV)]
+    outputs.append(pltpu.make_async_copy(gh, gh_hbm, osem.at[NV]))
+    for copy in inputs:
         copy.start()
+
+    def head_block(b):
+        stage[b] = jnp.dot(ft[b], grad[...], preferred_element_type=F32).astype(BF16)
+        outputs[b].start()
+
+    for b in range(4):
+        head_block(b)
+    for copy in inputs:
+        copy.wait()
     h = hid[...].astype(F32)
     inv_rms = lax.rsqrt(jnp.mean(h * h, axis=1, keepdims=True) + epsilon)
     dots = jnp.zeros((2, 1), F32)
@@ -535,13 +555,11 @@
     dots = dots / D
     for j in range(NJ):
         span = slice(j * SB, (j + 1) * SB)
-        gh_out[:, span] = (inv_rms * (rows[j] * gain[:, span] - h[:, span] * inv_rms * dots)).astype(BF16)
-    gcopy.wait()
-    for b in range(NV):
-        fcopies[b].wait()
-        stage[b] = jnp.dot(f[b], grad[...], preferred_element_type=F32).astype(BF16)
-        ocopies[b].start()
-    for copy in ocopies:
+        gh[:, span] = (inv_rms * (rows[j] * gain[:, span] - h[:, span] * inv_rms * dots)).astype(BF16)
+    outputs[NV].start()
+    for b in range(4, NV):
+        head_block(b)
+    for copy in outputs:
         copy.wait()
 
 
@@ -549,10 +567,13 @@
     vmem = pl.BlockSpec(memory_space=pltpu.VMEM)
     hbm = pl.BlockSpec(memory_space=pl.ANY)
     scratch = [
+        pltpu.VMEM((2, D), BF16),
+        pltpu.VMEM((1, D), F32),
+        pltpu.VMEM((1, ROWS), jnp.int32),
+        pltpu.VMEM((1, ROWS), jnp.int32),
         pltpu.VMEM((40, 128, COLS), BF16),
         pltpu.VMEM((1024, COLS), BF16),
         pltpu.VMEM((NC, NY, NV, NX, 16, CB), BF16),
-        pltpu.VMEM((NV, CB, ROWS), BF16),
         pltpu.VMEM((16, CB), F32),
         pltpu.VMEM((NZ, 16, CB), BF16),
         pltpu.VMEM((5, 128, 128), F32),
@@ -565,10 +586,9 @@
         pltpu.VMEM((NC, HALF, COLS), F32),
         pltpu.VMEM((NC, HALF, COLS), F32),
         pltpu.VMEM((ROWS, 128), F32),
-        pltpu.VMEM((NV, 8, ROWS), F32),
-        pltpu.VMEM((NX, 8, ROWS), F32),
-        pltpu.VMEM((NZ, 8, ROWS), F32),
-        pltpu.VMEM((ROWS, COLS), BF16),
+        pltpu.VMEM((NV, 4, ROWS), F32),
+        pltpu.VMEM((NX, 4, ROWS), F32),
+        pltpu.VMEM((NZ, 4, ROWS), F32),
         pltpu.VMEM((4, NY, NX, 16, SB), F32),
         pltpu.VMEM((4, NY, NX, 16, SB), F32),
         pltpu.VMEM((4, NY, NX, 16, SB), F32),
@@ -595,24 +615,24 @@
         pltpu.VMEM((NY, 2, SB), F32),
         pltpu.SemaphoreType.DMA((N_SEM,)),
         pltpu.SemaphoreType.DMA((N_SEM,)),
+        pltpu.SemaphoreType.DMA((4,)),
         pltpu.SemaphoreType.DMA,
         pltpu.SemaphoreType.DMA,
-        pltpu.SemaphoreType.DMA((2,)),
         pltpu.SemaphoreType.REGULAR,
     ]
     gain = norm_gain.reshape(1, D)
-    features, grad, rows = pl.pallas_call(
+    turned, grad, rows = pl.pallas_call(
         kernel,
         out_shape=(
-            jax.ShapeDtypeStruct((NV, CB, ROWS), BF16),
-            jax.ShapeDtypeStruct((ROWS, COLS), BF16),
-            jax.ShapeDtypeStruct((NJ, 2, SB), F32),
+            pltpu.VMEM((NV, CB, ROWS), BF16),
+            pltpu.VMEM((ROWS, COLS), BF16),
+            pltpu.VMEM((NJ, 2, SB), F32),
         ),
-        in_specs=[vmem, vmem, vmem, vmem, hbm, hbm],
-        out_specs=(hbm, hbm, vmem),
+        in_specs=[hbm] * 6,
+        out_specs=(vmem, vmem, vmem),
         scratch_shapes=scratch,
         compiler_params=pltpu.CompilerParams(
-            collective_id=0, has_side_effects=True, vmem_limit_bytes=60 * 2**20
+            collective_id=0, has_side_effects=True, vmem_limit_bytes=LIMIT * 2**20
         ),
         name="distill_head",
     )(
@@ -623,23 +643,22 @@
         head_weight.reshape(40, 128, COLS),
         teacher_logits.reshape(1024, COLS),
     )
-
     grad_hidden, grad_head = pl.pallas_call(
         finish_kernel,
         out_shape=(jax.ShapeDtypeStruct((2, D), BF16), jax.ShapeDtypeStruct((NV, CB, COLS), BF16)),
-        in_specs=[vmem, vmem, vmem, hbm, hbm],
-        out_specs=(vmem, hbm),
+        in_specs=[hbm, hbm, vmem, vmem, vmem],
+        out_specs=(hbm, hbm),
         scratch_shapes=[
-            pltpu.VMEM((NV, CB, ROWS), BF16),
-            pltpu.VMEM((ROWS, COLS), BF16),
+            pltpu.VMEM((2, D), BF16),
+            pltpu.VMEM((1, D), F32),
+            pltpu.VMEM((2, D), BF16),
             pltpu.VMEM((NV, CB, COLS), BF16),
-            pltpu.SemaphoreType.DMA,
-            pltpu.SemaphoreType.DMA((NV,)),
-            pltpu.SemaphoreType.DMA((NV,)),
+            pltpu.SemaphoreType.DMA((2,)),
+            pltpu.SemaphoreType.DMA((NV + 1,)),
         ],
-        compiler_params=pltpu.CompilerParams(vmem_limit_bytes=60 * 2**20),
+        compiler_params=pltpu.CompilerParams(vmem_limit_bytes=16 * 2**20),
         name="head_gradient",
-    )(hidden, gain, rows, features, grad)
+    )(hidden, gain, rows, turned, grad)
     return grad_hidden, grad_head.reshape(D, COLS)
 
 

time: 116 us -> 110 us (0.948)
  Pallas kernels: 115 us -> 109 us
    pallas_call x1, Pallas kernels: 8.89 us -> 4.04 us  [shards(): pl.pallas_call(finish_kernel, out_shape=(jax.ShapeDtypeStruct((2, D), BF1...]
    pallas_call x1, Pallas kernels: 106 us -> 104 us  [shards(): pl.pallas_call(kernel, out_shape=(pltpu.VMEM((NV, CB, ROWS), BF16), pltpu...]
where the time goes in v3:
time: 110 us; the launch traced here: 109 us
  Pallas kernels  109 us (99%)
    pallas_call x1, Pallas kernels, shards(): pl.pallas_call(kernel, out_shape=(pltpu.VMEM((NV, CB, ROWS), BF16), pltpu...  104 us
    pallas_call x1, Pallas kernels, shards(): pl.pallas_call(finish_kernel, out_shape=(jax.ShapeDtypeStruct((2, D), BF1...  4.04 us

profile of v3, /device:TPU:1, one launch (start us, length us, event | category | flops | bytes accessed | tf_op | source)
XLA Modules:
  0.0 109.2 jit_solution(15277819150568225642)
XLA Ops:
  0.6 0.0 copy-start
  0.6 0.0 copy-start.1
  0.7 104.5 %distill_head.1 = (bf16[8,640,512]{2,1,0:T(8,128)(2,1)S(1)}, bf16[512,512]{1,0:T(8,128)(2,1)S(1)}, f32[5,2,1024]{2,1,0:T(2,128)S(1)}) custom-call(bf16[2,5120]{1,0:T(2,128)(2,1)} %hid_hbm.3, f32[1,5120]{1,0:T(1,128)} %bitcast.6, s32[1,512]{1,0:T(1,128)} %bitcast.10, s32[1,512]{1,0:T(1,128)} %bitcast.11, bf16[40,128,512]{2,1,0:T(8,128)(2,1)} %bitcast.8, ...), custom_call_target="tpu_custom_call" | custom-call | tf_op jit(solution)/shard_map/distill_head/pallas_call | solution.py:624
  105.1 0.0 copy-done
  105.2 0.0 copy-done.1
  105.2 4.0 %head_gradient.1 = (bf16[2,5120]{1,0:T(2,128)(2,1)}, bf16[8,640,512]{2,1,0:T(8,128)(2,1)}) custom-call(bf16[2,5120]{1,0:T(2,128)(2,1)S(1)} %copy-done, f32[1,5120]{1,0:T(1,128)S(1)} %bitcast.7, f32[5,2,1024]{2,1,0:T(2,128)S(1)} %get-tuple-element.7.rows, bf16[8,640,512]{2,1,0:T(8,128)(2,1)S(1)} %get-tuple-element.8.ft, ...), custom_call_target="tpu_custom_call" | custom-call | tf_op jit(solution)/shard_map/head_gradient/pallas_call | solution.py:646
Async XLA Ops:
  0.6 104.5 %copy-start = (bf16[2,5120]{1,0:T(2,128)(2,1)S(1)}, bf16[2,5120]{1,0:T(2,128)(2,1)}, u32[]{:S(2)}) copy-start(bf16[2,5120]{1,0:T(2,128)(2,1)} %hid_hbm.3) | copy-start | bytes 61444
  0.6 104.5 %copy-start.1 = (f32[5120]{0:T(1024)S(1)}, f32[5120]{0:T(1024)}, u32[]{:S(2)}) copy-start(f32[5120]{0:T(1024)} %param.7) | copy-start | bytes 61444

commit v4 on v3

--- a/solution.py
+++ b/solution.py
@@ -17,7 +17,7 @@
 ROWS, D, CB, SB, COLS = 512, 5120, 640, 1024, 512
 HALF = ROWS // NC
 NJ = 5
-ORDER = (4, 0, 2, 1, 3)
+ORDER = (0, 2, 4, 1, 3)
 XFIRST, YFIRST = (0, 1), (2, 3)
 N_SEM = 240
 LIMIT = 55

time: 110 us -> 108 us (0.982)
  Pallas kernels: 109 us -> 107 us
    pallas_call x1, Pallas kernels: 104 us -> 103 us  [shards(): pl.pallas_call(kernel, out_shape=(pltpu.VMEM((NV, CB, ROWS), BF16), pltpu...]
where the time goes in v4:
time: 108 us; the launch traced here: 107 us
  Pallas kernels  107 us (99%)
    pallas_call x1, Pallas kernels, shards(): pl.pallas_call(kernel, out_shape=(pltpu.VMEM((NV, CB, ROWS), BF16), pltpu...  103 us
    pallas_call x1, Pallas kernels, shards(): pl.pallas_call(finish_kernel, out_shape=(jax.ShapeDtypeStruct((2, D), BF1...  4.04 us

profile of v4, /device:TPU:1, one launch (start us, length us, event | category | flops | bytes accessed | tf_op | source)
XLA Modules:
  0.0 107.3 jit_solution(5311948880675435848)
XLA Ops:
  0.6 0.0 copy-start
  0.6 0.0 copy-start.1
  0.7 102.6 %distill_head.1 = (bf16[8,640,512]{2,1,0:T(8,128)(2,1)S(1)}, bf16[512,512]{1,0:T(8,128)(2,1)S(1)}, f32[5,2,1024]{2,1,0:T(2,128)S(1)}) custom-call(bf16[2,5120]{1,0:T(2,128)(2,1)} %hid_hbm.3, f32[1,5120]{1,0:T(1,128)} %bitcast.6, s32[1,512]{1,0:T(1,128)} %bitcast.10, s32[1,512]{1,0:T(1,128)} %bitcast.11, bf16[40,128,512]{2,1,0:T(8,128)(2,1)} %bitcast.8, ...), custom_call_target="tpu_custom_call" | custom-call | tf_op jit(solution)/shard_map/distill_head/pallas_call | solution.py:624
  103.2 0.0 copy-done
  103.2 0.0 copy-done.1
  103.2 4.0 %head_gradient.1 = (bf16[2,5120]{1,0:T(2,128)(2,1)}, bf16[8,640,512]{2,1,0:T(8,128)(2,1)}) custom-call(bf16[2,5120]{1,0:T(2,128)(2,1)S(1)} %copy-done, f32[1,5120]{1,0:T(1,128)S(1)} %bitcast.7, f32[5,2,1024]{2,1,0:T(2,128)S(1)} %get-tuple-element.7.rows, bf16[8,640,512]{2,1,0:T(8,128)(2,1)S(1)} %get-tuple-element.8.ft, ...), custom_call_target="tpu_custom_call" | custom-call | tf_op jit(solution)/shard_map/head_gradient/pallas_call | solution.py:646
Async XLA Ops:
  0.6 102.6 %copy-start = (bf16[2,5120]{1,0:T(2,128)(2,1)S(1)}, bf16[2,5120]{1,0:T(2,128)(2,1)}, u32[]{:S(2)}) copy-start(bf16[2,5120]{1,0:T(2,128)(2,1)} %hid_hbm.3) | copy-start | bytes 61444
  0.6 102.6 %copy-start.1 = (f32[5120]{0:T(1024)S(1)}, f32[5120]{0:T(1024)}, u32[]{:S(2)}) copy-start(f32[5120]{0:T(1024)} %param.7) | copy-start | bytes 61444

commit v5 on v4

--- a/solution.py
+++ b/solution.py
@@ -21,7 +21,7 @@
 XFIRST, YFIRST = (0, 1), (2, 3)
 N_SEM = 240
 LIMIT = 55
-FIRST = 7
+FIRST = 15
 SPLIT = 6
 
 
@@ -335,7 +335,8 @@
             source = mod(here + count - k, count)
             return links.copy(buffer.at[source], buffer.at[source], device(source), start + k)
 
-        loop(count - 1, lambda k: out(k + 1).start())
+        for k in sorted(range(1, count), key=lambda k: -min(k, count - k)):
+            out(k).start()
         for b in blocks:
             ft[b] = f[:, :, b].reshape(ROWS, CB).T
         loop(count - 1, lambda k: arrival(k + 1).wait_recv())
@@ -458,12 +459,17 @@
         else:
             stage1[j] = Line()
 
-    for n, j in enumerate(ORDER):
+    def other_half(j):
         partial(j, 1 - c, poz if j == 4 else po)
         go(core_links[j])
+
+    other_half(ORDER[0])
+    for n, j in enumerate(ORDER):
+        if n + 1 < len(ORDER):
+            other_half(ORDER[n + 1])
         partial(j, c, psz if j == 4 else ps)
-        if n:
-            begin(ORDER[n - 1])
+        if n + 1 < len(ORDER):
+            begin(j)
     begin(ORDER[-1])
 
     for j in (0, 2, 4, 1, 3):
@@ -480,7 +486,8 @@
             other = mod(here + count - k, count)
             return links.copy(source.at[other], buffer.at[other], device(other), start + k)
 
-        loop(count - 1, lambda k: out(k + 1).start())
+        for k in sorted(range(1, count), key=lambda k: -min(k, count - k)):
+            out(k).start()
         buffer[here] = source[here]
         flushes.append(lambda: loop(count - 1, lambda k: out(k + 1).wait_send()))
         return lambda: loop(count - 1, lambda k: arrival(k + 1).wait_recv())

time: 108 us -> 107 us (level)
  Pallas kernels: 107 us -> 105 us
    pallas_call x1, Pallas kernels: 103 us -> 101 us  [shards(): pl.pallas_call(kernel, out_shape=(pltpu.VMEM((NV, CB, ROWS), BF16), pltpu...]
where the time goes in v5:
time: 107 us; the launch traced here: 106 us
  Pallas kernels  105 us (98%)
    pallas_call x1, Pallas kernels, shards(): pl.pallas_call(kernel, out_shape=(pltpu.VMEM((NV, CB, ROWS), BF16), pltpu...  101 us
    pallas_call x1, Pallas kernels, shards(): pl.pallas_call(finish_kernel, out_shape=(jax.ShapeDtypeStruct((2, D), BF1...  4.04 us

profile of v5, /device:TPU:1, one launch (start us, length us, event | category | flops | bytes accessed | tf_op | source)
XLA Modules:
  0.0 105.9 jit_solution(7625176945402891974)
XLA Ops:
  0.6 0.0 copy-start
  0.6 0.0 copy-start.1
  0.7 101.1 %distill_head.1 = (bf16[8,640,512]{2,1,0:T(8,128)(2,1)S(1)}, bf16[512,512]{1,0:T(8,128)(2,1)S(1)}, f32[5,2,1024]{2,1,0:T(2,128)S(1)}) custom-call(bf16[2,5120]{1,0:T(2,128)(2,1)} %hid_hbm.3, f32[1,5120]{1,0:T(1,128)} %bitcast.6, s32[1,512]{1,0:T(1,128)} %bitcast.10, s32[1,512]{1,0:T(1,128)} %bitcast.11, bf16[40,128,512]{2,1,0:T(8,128)(2,1)} %bitcast.8, ...), custom_call_target="tpu_custom_call" | custom-call | tf_op jit(solution)/shard_map/distill_head/pallas_call | solution.py:631
  101.8 0.0 copy-done
  101.8 0.0 copy-done.1
  101.8 4.0 %head_gradient.1 = (bf16[2,5120]{1,0:T(2,128)(2,1)}, bf16[8,640,512]{2,1,0:T(8,128)(2,1)}) custom-call(bf16[2,5120]{1,0:T(2,128)(2,1)S(1)} %copy-done, f32[1,5120]{1,0:T(1,128)S(1)} %bitcast.7, f32[5,2,1024]{2,1,0:T(2,128)S(1)} %get-tuple-element.7.rows, bf16[8,640,512]{2,1,0:T(8,128)(2,1)S(1)} %get-tuple-element.8.ft, ...), custom_call_target="tpu_custom_call" | custom-call | tf_op jit(solution)/shard_map/head_gradient/pallas_call | solution.py:653
Async XLA Ops:
  0.6 101.2 %copy-start = (bf16[2,5120]{1,0:T(2,128)(2,1)S(1)}, bf16[2,5120]{1,0:T(2,128)(2,1)}, u32[]{:S(2)}) copy-start(bf16[2,5120]{1,0:T(2,128)(2,1)} %hid_hbm.3) | copy-start | bytes 61444
  0.6 101.2 %copy-start.1 = (f32[5120]{0:T(1024)S(1)}, f32[5120]{0:T(1024)}, u32[]{:S(2)}) copy-start(f32[5120]{0:T(1024)} %param.7) | copy-start | bytes 61444
